TPU v7x, 768 devices: a whole 4x8x12 slice. The times are simulated.
768 devices in a mesh: batch: 96 (over z_lo, y, core), tensor: 8 (over z_hi, x).
Axes of the slice: x: 4, y: 8, z: 12 (z_hi: 2, z_lo: 6; z = z_hi * 6 + z_lo), core: 2. Of those that a mesh axis runs over, the one named last changes fastest.
Arguments:
- audio_hidden: bfloat16 [12288, 4096], P('batch'), may hold values from -9 to 9
- head_in: bfloat16 [4096, 1536], P(None, 'tensor'), may hold values from -1 to 1
- head_out: bfloat16 [1536, 1536], P('tensor'), may hold values from -1 to 1
- text_embed: bfloat16 [12288, 1536], P('batch'), may hold values from -6 to 6
- log_scale: float32 [], replicated, may hold values from 4.8 to 5.3
- pair_index: int32 [12288], P('batch'), may hold values from 0 to 12287, each once
- valid_count: int32 [96], replicated, may hold values from 32 to 128, as said below
Outputs:
- row_loss: float32 [12288], P(('batch', 'tensor'))
- grad_audio: float32 [12288, 1536], P(('batch', 'tensor'))
Inputs may be any that keep to these rules, and one draw needn't show every extreme that they name: `valid_count`: one batch block has all 128 rows valid in every draw.
All inputs are finite; a program needn't handle non-finite values.
Results may differ from a plain program's by a relative error of at most 0.0064.
Values may be sent and summed in bfloat16 or wider, within the bound.
No kernel may reach another device: no remote copies, remote signals or barrier semaphores. Data moves between devices by JAX's collectives and lax.ppermute only.
A program may use at most 32 MiB of HBM per device.

v0:
```python
import jax
import jax.numpy as jnp
from jax import lax
from jax.sharding import PartitionSpec as P


def merged(part, axis, combine):
    gathered = jax.tree.map(lambda a: lax.all_gather(a, axis), part)

    def take(source):
        return jax.tree.map(lambda a: lax.dynamic_index_in_dim(a, source, 0, False), gathered)

    return lax.fori_loop(
        1, lax.axis_size(axis), lambda source, state: combine(state, take(source)), take(0)
    )


def unit_rows(values):
    return values * lax.rsqrt(jnp.sum(values * values, axis=1, keepdims=True) + 1e-06)


def scores(text_unit, columns, scale):
    return scale * jnp.einsum("rd,cd->rc", text_unit, columns, preferred_element_type=jnp.float32)


def combine_stats(first, second):
    top_new = jnp.maximum(first[0], second[0])
    mass = first[1] * jnp.exp(first[0] - top_new) + second[1] * jnp.exp(second[0] - top_new)
    return (top_new, mass, first[2] + second[2])


def block_stats(logits, target_col, owned, start):
    width = logits.shape[1]
    top = jnp.max(logits, axis=1)
    mass = jnp.sum(jnp.exp(logits - top[:, None]), axis=1)
    offset = target_col - start
    inside = owned & (offset >= 0) & (offset < width)
    value = jnp.take_along_axis(logits, jnp.clip(offset, 0, width - 1)[:, None], axis=1)[:, 0]
    return (top, mass, jnp.where(inside, value, 0.0))


def block_terms(logits, total, target_col, owned, valid, text_unit):
    width = logits.shape[1]
    columns = jnp.arange(width, dtype=jnp.int32)
    onehot = ((columns[None, :] == target_col[:, None]) & owned[:, None]).astype(jnp.float32)
    weights = jnp.where(valid[:, None], jnp.exp(logits - total[:, None]) - onehot, 0.0).astype(
        jnp.bfloat16
    )
    return jnp.einsum("rc,rd->cd", weights, text_unit, preferred_element_type=jnp.float32)


def on_device(audio_hidden, head_in, head_out, text_embed, log_scale, pair_index, valid_count):
    row_count = audio_hidden.shape[0]
    groups = lax.axis_size("tensor")
    share = row_count // groups
    tensor_pos = lax.axis_index("tensor")
    batch_pos = lax.axis_index("batch")
    pre_act = jnp.dot(audio_hidden, head_in, preferred_element_type=jnp.float32)
    hidden = jax.nn.gelu(pre_act, approximate=False).astype(jnp.bfloat16)
    summed = lax.psum(jnp.dot(hidden, head_out, preferred_element_type=jnp.float32), "tensor")
    raw = lax.dynamic_slice_in_dim(summed, tensor_pos * share, share, 0)
    audio_unit = unit_rows(raw).astype(jnp.bfloat16)
    text_unit = unit_rows(text_embed.astype(jnp.float32)).astype(jnp.bfloat16)
    scale = jnp.exp(log_scale)
    valid = jnp.arange(row_count, dtype=jnp.int32) < valid_count[batch_pos]
    owner_block = pair_index // row_count
    within = pair_index % row_count
    owned = within // share == tensor_pos
    target_col = owner_block * share + within % share
    gathered = lax.all_gather(audio_unit, "batch", axis=0, tiled=True)
    logits = scores(text_unit, gathered, scale)
    local_stats = block_stats(logits, target_col, owned, 0)
    top, mass, picked = merged(local_stats, "tensor", combine_stats)
    total = top + jnp.log(mass)
    losses = jnp.where(valid, total - picked, 0.0)
    row_loss = lax.dynamic_slice_in_dim(losses, tensor_pos * share, share, 0)
    terms = block_terms(logits, total, target_col, owned, valid, text_unit)
    grad_audio = scale * lax.psum_scatter(terms, "batch", scatter_dimension=0, tiled=True)
    return (row_loss, grad_audio)


def solution(mesh):
    placed = (
        P("batch", None),
        P(None, "tensor"),
        P("tensor", None),
        P("batch", None),
        P(),
        P("batch"),
        P(),
    )
    return jax.shard_map(
        on_device,
        mesh=mesh,
        in_specs=placed,
        out_specs=(P(("batch", "tensor")), P(("batch", "tensor"), None)),
        check_vma=False,
    )
```

profile of v0, /device:TPU:1, one launch (start us, length us, event | category | flops | bytes accessed | tf_op | source)
XLA Modules:
  0.0 1009.3 jit_solution(2922073057447604389)
XLA Ops:
  7.2 0.0 copy-start
  7.2 0.0 copy-start.3
  7.2 0.0 copy-start.2
  7.2 0.0 copy-start.1
  7.2 0.0 all-reduce.2.cloned.1.call-start
  7.3 1.3 copy-done
  8.6 3.5 fusion.28
  12.1 0.0 all-reduce.2.cloned.1.call-update
  12.1 0.0 all-gather.8.cloned.1.call-start
  12.2 147.4 %all-reduce.2.cloned.1.call-done = f32[128,1536]{1,0:T(8,128)} async-done(((f32[128,1536]{1,0:T(8,128)}), f32[128,1536]{1,0:T(8,128)}) %all-reduce.2.cloned.1.call-update) | async-done | bytes 786448 | tf_op jit(solution)/shard_map/psum | solution.py:60
  159.5 1.0 multiply_reduce_fusion
  160.6 1.6 multiply_convert_fusion
  162.2 0.0 all-gather.8.cloned.1.call-update
  162.2 0.0 reduce-scatter.2.cloned.1.call-start
  162.9 0.0 copy-done.3
  162.9 0.6 dynamic_slice.49
  163.6 0.7 iota_compare_fusion.1
  164.3 0.0 copy-done.2
  164.3 0.0 copy-done.1
  164.3 0.2 fusion.7
  164.5 173.0 %all-gather.8.cloned.1.call-done = bf16[1536,1536]{1,0:T(8,128)(2,1)} async-done(((bf16[16,1536]{1,0:T(8,128)(2,1)}), bf16[1536,1536]{1,0:T(8,128)(2,1)}) %all-gather.8.cloned.1.call-update) | async-done | bytes 4718608 | tf_op jit(solution)/shard_map/all_gather | solution.py:70
  337.5 4.1 fusion.98
  341.6 1.5 gather_fusion
  343.1 0.3 exponential_reduce_fusion
  343.3 32.0 %all-gather.4 = f32[8,1,128]{2,1,0:T(1,128)S(1)} all-gather(f32[1,1,128]{2,1,0:T(1,128)S(1)} %bitcast.47), channel_id=3, replica_groups=mesh['batch'=96,'tensor'=8] {'tensor'}, dimensions={0}, use_global_device_ids=true | all-gather | bytes 4608 | tf_op jit(solution)/shard_map/all_gather | solution.py:8
  375.4 24.1 %all-gather.5 = f32[8,1,128]{2,1,0:T(1,128)S(1)} all-gather(f32[1,1,128]{2,1,0:T(1,128)S(1)} %get-tuple-element.201), channel_id=4, replica_groups=mesh['batch'=96,'tensor'=8] {'tensor'}, dimensions={0}, use_global_device_ids=true | all-gather | bytes 4608 | tf_op jit(solution)/shard_map/all_gather | solution.py:8
  399.5 25.6 %all-gather.3 = f32[8,1,128]{2,1,0:T(1,128)S(1)} all-gather(f32[1,1,128]{2,1,0:T(1,128)S(1)} %bitcast.46), channel_id=2, replica_groups=mesh['batch'=96,'tensor'=8] {'tensor'}, dimensions={0}, use_global_device_ids=true | all-gather | bytes 4608 | tf_op jit(solution)/shard_map/all_gather | solution.py:8
  425.1 0.3 while.19
  425.4 0.7 subtract_select_fusion.1
  426.0 5.3 fusion.10
  431.3 0.0 reduce-scatter.2.cloned.1.call-update
  431.4 0.6 dynamic_slice.54
  431.9 569.3 %reduce-scatter.2.cloned.1.call-done = f32[16,1536]{1,0:T(8,128)} async-done(((f32[1536,1536]{1,0:T(8,128)}), f32[16,1536]{1,0:T(8,128)}) %reduce-scatter.2.cloned.1.call-update) | async-done | bytes 98320 | tf_op jit(solution)/shard_map/reduce_scatter | solution.py:78
  1001.3 1.5 broadcast_multiply_fusion
  (17 shorter events, 0.3 us)
Async XLA Ops:
  7.2 1.4 copy-start
  7.2 155.8 %copy-start.3 = (s32[96]{0:T(128)S(1)}, s32[96]{0:T(128)}, u32[]{:S(2)}) copy-start(s32[96]{0:T(128)} %param.15) | copy-start | bytes 1156
  7.2 157.1 %copy-start.2 = (s32[128]{0:T(128)S(1)}, s32[128]{0:T(128)}, u32[]{:S(2)}) copy-start(s32[128]{0:T(128)} %param.14) | copy-start | bytes 1540
  7.2 157.1 %copy-start.1 = (bf16[128,1536]{1,0:T(8,128)(2,1)S(1)}, bf16[128,1536]{1,0:T(8,128)(2,1)}, u32[]{:S(2)}) copy-start(bf16[128,1536]{1,0:T(8,128)(2,1)} %param.12) | copy-start | bytes 1179652
  7.2 152.3 %all-reduce.2.cloned.1.call-start = ((), (), s32[]{:S(2)}) async-start(), calls=%async_computation.1 | async-start | bytes 1572864 | tf_op jit(solution)/shard_map/psum | solution.py:60
  12.1 325.4 %all-gather.8.cloned.1.call-start = ((), (), s32[]{:S(2)}) async-start(), calls=%async_computation.2 | async-start | bytes 4767744 | tf_op jit(solution)/shard_map/all_gather | solution.py:70
  162.2 839.1 %reduce-scatter.2.cloned.1.call-start = ((), (), s32[]{:S(2)}) async-start(), calls=%async_computation.3 | async-start | bytes 9535488 | tf_op jit(solution)/shard_map/reduce_scatter | solution.py:78
Sparse Core Ops, SparseCore 0:
  12.2 147.2 all-reduce.1
  162.9 174.5 all-gather.7
  431.5 569.7 reduce-scatter.1
where the time goes:
time: 1020 us; the launch traced here: 1010 us
  waiting for transfers between devices  890 us (87%)
  blocking collectives  81.7 us (8%)
  between operations  14.6 us (1%)
  matrix products  12.9 us (1%)
    reduce_scatter x1, waiting for transfers between devices, on_device(): lax.psum_scatter(terms, 'batch', scatter_dimension=0, tiled=True)  569 us
    all_gather x1, waiting for transfers between devices, on_device(): gathered = lax.all_gather(audio_unit, 'batch', axis=0, tiled=True)  173 us
    psum x1, waiting for transfers between devices, on_device(): lax.psum(jnp.dot(hidden, head_out, preferred_element_type=jnp.float32), '...  147 us
    all_gather x3, blocking collectives, merged(): gathered = jax.tree.map(lambda a: lax.all_gather(a, axis), part)  81.7 us
  transfers between devices with their start and end apart: 3, of which 3 were waited for; matrix products, arithmetic and copies ran while one was open for 0% of the time, Pallas kernels for 0%

commit v1 on v0

v1 whole, which is shorter than its diff:
```python
import jax
import jax.numpy as jnp
from jax import lax
from jax.sharding import Mesh, PartitionSpec as P

BATCH = ("zl", "y", "c")
TENSOR = ("zh", "x")
BF16 = jnp.bfloat16
F32 = jnp.float32


def unit_rows(values):
    return values * lax.rsqrt(jnp.sum(values * values, axis=1, keepdims=True) + 1e-06)


def swapped(value, axis):
    return lax.ppermute(value, axis, [(0, 1), (1, 0)])


def spread(value, axis, count):
    chunks = jnp.broadcast_to(value[None], (count,) + value.shape)
    return lax.all_to_all(chunks, axis, 0, 0)


def log_sum_exp(values, axis):
    top = jnp.max(values, axis=axis)
    return top + jnp.log(jnp.sum(jnp.exp(values - jnp.expand_dims(top, axis)), axis=axis))


def on_device(audio_hidden, head_in, head_out, text_embed, log_scale, pair_index, valid_count):
    rows, width = text_embed.shape
    n_zl, n_y, n_zh, n_x = (lax.axis_size(a) for a in ("zl", "y", "zh", "x"))
    zl, y, c, zh, x = (lax.axis_index(a) for a in ("zl", "y", "c", "zh", "x"))
    share = rows // (n_zh * n_x)
    scale = jnp.exp(log_scale)

    text_unit = unit_rows(text_embed.astype(F32)).astype(BF16)
    low = jnp.broadcast_to((pair_index % rows).astype(BF16)[None], (rows // 2, rows))
    high = jnp.broadcast_to((pair_index // rows).astype(BF16)[None], (rows // 2, rows))
    packed = jnp.concatenate([text_unit, jnp.concatenate([low, high], 0)], axis=1)
    text_all = lax.all_gather(packed, "y", axis=0, tiled=True)

    pre_act = jnp.dot(audio_hidden, head_in, preferred_element_type=F32)
    hidden = jax.nn.gelu(pre_act, approximate=False).astype(BF16)
    partial = jnp.dot(hidden, head_out, preferred_element_type=F32).astype(BF16)
    partial = partial.reshape(n_zh, n_x, share, width).transpose(1, 0, 2, 3)
    partial = lax.all_to_all(partial, "x", 0, 0)
    halves = jnp.sum(partial.astype(F32), axis=0)
    mine = jnp.where(zh == 0, halves[0], halves[1])
    other = jnp.where(zh == 0, halves[1], halves[0])
    raw = mine + swapped(other.astype(BF16), "zh").astype(F32)
    audio_unit = unit_rows(raw).astype(BF16)

    own = spread(audio_unit, "zl", n_zl).reshape(n_zl * share, width)
    audio = jnp.concatenate([own, swapped(own, "c")], axis=0)
    half = n_zl * share

    text = text_all[:, :width]
    extra = text_all[:, width:].reshape(n_y, rows, rows)
    low = extra[:, 0].astype(jnp.int32)
    high = extra[:, rows // 2].astype(jnp.int32)
    pair_c = high % 2
    pair_y = (high // 2) % n_y
    pair_zl = high // (2 * n_y)
    held = (pair_y == y) & (low // share == zh * n_x + x)
    column = jnp.where(pair_c == c, 0, half) + pair_zl * share + low % share
    column = jnp.where(held, column, -1).reshape(1, n_y * rows)
    onehot = lax.broadcasted_iota(jnp.int32, (2 * half, n_y * rows), 0) == column

    logits = scale * jnp.einsum("ae,te->at", audio, text, preferred_element_type=F32)
    local = log_sum_exp(logits, 0).reshape(n_y, rows)
    picked = jnp.sum(jnp.where(onehot, logits, 0.0), axis=0).reshape(n_y, rows)

    stats = spread(jnp.concatenate([local, picked], 0), ("y", "x"), n_y * n_x)
    local = log_sum_exp(stats[:, :n_y], 0)
    picked = jnp.sum(stats[:, n_y:], axis=0)
    both = swapped(jnp.concatenate([local, picked], 0), "zh")
    total = log_sum_exp(jnp.stack([local, both[:n_y]]), 0)
    picked = picked + both[n_y:]

    counts = lax.dynamic_slice_in_dim(valid_count.reshape(n_zl, n_y, 2), zl, 1, 0)[0]
    counts = jnp.where(c == 0, counts[:, 0], counts[:, 1])
    valid = lax.broadcasted_iota(jnp.int32, (n_y, rows), 1) < counts[:, None]
    losses = jnp.where(valid, total - picked, 0.0)
    losses = lax.dynamic_index_in_dim(losses, y, 0, False)
    row_loss = lax.dynamic_slice_in_dim(losses, (zh * n_x + x) * share, share, 0)

    weights = jnp.exp(logits - total.reshape(1, -1)) - onehot.astype(F32)
    weights = jnp.where(valid.reshape(1, -1), weights, 0.0).astype(BF16)
    terms = jnp.einsum("at,te->ae", weights, text, preferred_element_type=F32)
    kept = terms[:half] + swapped(terms[half:].astype(BF16), "c").astype(F32)
    parts = lax.all_to_all(kept.astype(BF16).reshape(n_zl, share, width), "zl", 0, 0)
    grad_audio = scale * jnp.sum(parts.astype(F32), axis=0)
    return (row_loss, grad_audio)


def build(mesh):
    placed = (
        P(BATCH, None),
        P(None, TENSOR),
        P(TENSOR, None),
        P(BATCH, None),
        P(),
        P(BATCH),
        P(),
    )
    return jax.shard_map(
        on_device,
        mesh=mesh,
        in_specs=placed,
        out_specs=(P(BATCH + TENSOR), P(BATCH + TENSOR, None)),
        check_vma=False,
    )


def solution(mesh):
    return build(Mesh(mesh.devices.reshape(6, 8, 2, 2, 4), BATCH + TENSOR))
```

time: 1020 us -> 146 us (0.14)
  waiting for transfers between devices: 890 us -> 48.2 us
  blocking collectives: 81.7 us -> 0 us
  starting transfers between devices: 0.12 us -> 64 us
    reduce_scatter x1 -> x0, waiting for transfers between devices: 569 us -> none  [on_device(): lax.psum_scatter(terms, 'batch', scatter_dimension=0, tiled=True)]
    all_gather x1, waiting for transfers between devices: 173 us -> 3.51 us  [on_device(): text_all = lax.all_gather(packed, 'y', axis=0, tiled=True)]
    psum x1 -> x0, waiting for transfers between devices: 147 us -> none  [on_device(): lax.psum(jnp.dot(hidden, head_out, preferred_element_type=jnp.float32), '...]
    all_gather x3 -> x0, blocking collectives: 81.7 us -> none  [merged(): gathered = jax.tree.map(lambda a: lax.all_gather(a, axis), part)]
    all_to_all x0 -> x4, waiting for transfers between devices: none -> 41 us  [the longest x2 21.4 us: spread(): return lax.all_to_all(chunks, axis, 0, 0)]
    ppermute x0 -> x4, starting transfers between devices: none -> 37.6 us  [swapped(): return lax.ppermute(value, axis, [(0, 1), (1, 0)])]
    all_to_all x0 -> x4, starting transfers between devices: none -> 26.4 us  [the longest x2 13.9 us: spread(): return lax.all_to_all(chunks, axis, 0, 0)]
  transfers between devices with their start and end apart: 3 -> 9, of which waited for: 3 -> 8; matrix products, arithmetic and copies ran while one was open for 0% -> 4% of each run, Pallas kernels for 0% -> 0%
where the time goes in v1:
time: 146 us; the launch traced here: 145 us
  starting transfers between devices  64 us (44%)
  waiting for transfers between devices  48.2 us (33%)
  between operations  15 us (10%)
  matrix products  8.06 us (6%)
  other arithmetic  6.16 us (4%)
  local copies, waits for them, and re-layouts  4.07 us (3%)
    ppermute x4, starting transfers between devices, swapped(): return lax.ppermute(value, axis, [(0, 1), (1, 0)])  37.6 us
    all_to_all x2, waiting for transfers between devices, spread(): return lax.all_to_all(chunks, axis, 0, 0)  21.4 us
    all_to_all x2, starting transfers between devices, spread(): return lax.all_to_all(chunks, axis, 0, 0)  13.9 us
    all_to_all x1, waiting for transfers between devices, on_device(): lax.all_to_all(kept.astype(BF16).reshape(n_zl, share, width), 'zl', 0, 0)  13.4 us
    all_to_all x1, starting transfers between devices, on_device(): lax.all_to_all(kept.astype(BF16).reshape(n_zl, share, width), 'zl', 0, 0)  7.63 us
    all_to_all x1, waiting for transfers between devices, on_device(): partial = lax.all_to_all(partial, 'x', 0, 0)  6.23 us
    all_to_all x1, starting transfers between devices, on_device(): partial = lax.all_to_all(partial, 'x', 0, 0)  4.84 us
    ppermute x4, waiting for transfers between devices, swapped(): return lax.ppermute(value, axis, [(0, 1), (1, 0)])  3.64 us
  transfers between devices with their start and end apart: 9, of which 8 were waited for; matrix products, arithmetic and copies ran while one was open for 4% of the time, Pallas kernels for 0%

profile of v1, /device:TPU:1, one launch (start us, length us, event | category | flops | bytes accessed | tf_op | source)
XLA Modules:
  0.0 145.4 jit_solution(8624526020459547193)
XLA Ops:
  7.2 0.0 copy-start
  7.2 0.0 copy-start.2
  7.2 0.0 all-gather.2.cloned.1.call-start
  7.2 1.3 fusion.7
  8.5 0.7 fusion.79
  9.2 1.1 fusion.8
  10.4 0.8 maximum_maximum_fusion
  11.2 0.0 all-gather.2.cloned.1.call-update
  11.2 0.0 copy-done
  11.2 0.0 copy-done.2
  11.2 2.3 %convolution_convert_fusion = bf16[128,1536]{1,0:T(8,128)(2,1)S(1)} fusion(bf16[192,1536]{1,0:T(8,128)(2,1)} %param.9, bf16[128,4096]{1,0:T(8,128)(2,1)S(1)} %copy-done.2, bf16[4096,192]{0,1:T(8,128)(2,1)S(1)} %copy-done), kind=kOutput, calls=%fused_computation.4 | convolution fusion | flops 278618112 | bytes 3604480 | tf_op jit(solution)/shard_map/dot_general | solution.py:45
  13.5 0.8 copy.16
  14.3 4.8 %all-to-all-start = ((bf16[4,2,16,1536]{3,2,1,0:T(8,128)(2,1)}), bf16[4,2,16,1536]{3,2,1,0:T(8,128)(2,1)S(1)}, u32[]{:S(2)}, u32[]{:S(2)}) async-start(bf16[4,2,16,1536]{3,2,1,0:T(8,128)(2,1)} %bitcast.34), calls=%async_computation | async-start | bytes 786432 | tf_op jit(solution)/shard_map/all_to_all | solution.py:47
  19.1 6.2 %all-to-all-done = bf16[4,2,16,1536]{3,2,1,0:T(8,128)(2,1)S(1)} async-done(((bf16[4,2,16,1536]{3,2,1,0:T(8,128)(2,1)}), bf16[4,2,16,1536]{3,2,1,0:T(8,128)(2,1)S(1)}, u32[]{:S(2)}, u32[]{:S(2)}) %all-to-all-start) | async-done | bytes 393248 | tf_op jit(solution)/shard_map/all_to_all | solution.py:47
  25.4 0.1 convert_reduce_fusion
  25.4 15.5 %collective-permute-start = (bf16[16,1536]{1,0:T(8,128)(2,1)S(1)}, bf16[16,1536]{1,0:T(8,128)(2,1)S(1)}, u32[]{:S(2)}, u32[]{:S(2)}) collective-permute-start(bf16[16,1536]{1,0:T(8,128)(2,1)S(1)} %fusion.28), channel_id=1, source_target_pairs={{0,4},{4,0},{1,5},{5,1},{2,6},{6,2},{3,7},{7,3},{8,12},{12,8},{9,1... | collective-permute-start | bytes 147464 | tf_op jit(solution)/shard_map/ppermute | solution.py:17
  40.9 1.5 %collective-permute-done = bf16[16,1536]{1,0:T(8,128)(2,1)S(1)} collective-permute-done((bf16[16,1536]{1,0:T(8,128)(2,1)S(1)}, bf16[16,1536]{1,0:T(8,128)(2,1)S(1)}, u32[]{:S(2)}, u32[]{:S(2)}) %collective-permute-start) | collective-permute-done | bytes 49184 | tf_op jit(solution)/shard_map/ppermute | solution.py:17
  42.4 0.1 multiply_reduce_fusion
  42.6 0.1 multiply_convert_fusion
  42.7 0.7 broadcast_in_dim.29
  43.4 6.9 %all-to-all-start.1 = ((bf16[6,16,1536]{2,1,0:T(8,128)(2,1)}), bf16[6,16,1536]{2,1,0:T(8,128)(2,1)S(1)}, u32[]{:S(2)}, u32[]{:S(2)}) async-start(bf16[6,16,1536]{2,1,0:T(8,128)(2,1)} %broadcast_in_dim.29), calls=%async_computation.1 | async-start | bytes 589824 | tf_op jit(solution)/shard_map/all_to_all | solution.py:22
  51.0 10.5 %all-to-all-done.1 = bf16[6,16,1536]{2,1,0:T(8,128)(2,1)S(1)} async-done(((bf16[6,16,1536]{2,1,0:T(8,128)(2,1)}), bf16[6,16,1536]{2,1,0:T(8,128)(2,1)S(1)}, u32[]{:S(2)}, u32[]{:S(2)}) %all-to-all-start.1) | async-done | bytes 294944 | tf_op jit(solution)/shard_map/all_to_all | solution.py:22
  61.5 6.4 %collective-permute-start.1 = (bf16[96,1536]{1,0:T(8,128)(2,1)S(1)}, bf16[96,1536]{1,0:T(8,128)(2,1)S(1)}, u32[]{:S(2)}, u32[]{:S(2)}) collective-permute-start(bf16[96,1536]{1,0:T(8,128)(2,1)S(1)} %bitcast.36), channel_id=1, source_target_pairs={{0,8},{8,0},{1,9},{9,1},{2,10},{10,2},{3,11},{11,3},{4,12},{12,4},... | collective-permute-start | bytes 884744 | tf_op jit(solution)/shard_map/ppermute | solution.py:17
  67.9 3.5 %all-gather.2.cloned.1.call-done = bf16[1024,1664]{1,0:T(8,128)(2,1)} async-done(((bf16[128,1664]{1,0:T(8,128)(2,1)}), bf16[1024,1664]{1,0:T(8,128)(2,1)}) %all-gather.2.cloned.1.call-update) | async-done | bytes 3407888 | tf_op jit(solution)/shard_map/all_gather | solution.py:41
  71.4 1.0 slice.62
  72.4 0.0 collective-permute-done.1
  72.4 3.1 %fusion.113 = (f32[1024]{0:T(1024)S(1)}, f32[192,1024]{1,0:T(8,128)S(1)}) fusion(bf16[1024,1664]{1,0:T(8,128)(2,1)} %all-gather.2.cloned.1.call-done, bf16[96,1536]{1,0:T(8,128)(2,1)S(1)} %collective-permute-done.1, bf16[96,1536]{1,0:T(8,128)(2,1)S(1)} %bitcast.37, f32[]{:T(128)S(6)} %exp.15), kind=kOutput, calls=%fused_computation.180 | convolution fusion | flops 605551616 | bytes 4526084 | tf_op jit(solution)/shard_map/ae,te->at/dot_general | solution.py:70
  75.5 0.0 copy-start.1
  75.5 0.2 exponential_reduce_fusion
  75.8 0.7 broadcast_in_dim.35
  76.5 7.0 %all-to-all-start.2 = ((f32[32,16,128]{2,1,0:T(8,128)}), f32[32,16,128]{2,1,0:T(8,128)S(1)}, u32[]{:S(2)}, u32[]{:S(2)}) async-start(f32[32,16,128]{2,1,0:T(8,128)} %broadcast_in_dim.35), calls=%async_computation.2 | async-start | bytes 524288 | tf_op jit(solution)/shard_map/all_to_all | solution.py:22
  83.5 0.0 copy-done.1
  83.5 0.1 reshape.214
  83.7 0.1 copy.13
  83.7 10.9 %all-to-all-done.2 = f32[32,16,128]{2,1,0:T(8,128)S(1)} async-done(((f32[32,16,128]{2,1,0:T(8,128)}), f32[32,16,128]{2,1,0:T(8,128)S(1)}, u32[]{:S(2)}, u32[]{:S(2)}) %all-to-all-start.2) | async-done | bytes 262176 | tf_op jit(solution)/shard_map/all_to_all | solution.py:22
  94.8 10.5 %collective-permute-start.2 = (f32[16,128]{1,0:T(8,128)S(1)}, f32[16,128]{1,0:T(8,128)S(1)}, u32[]{:S(2)}, u32[]{:S(2)}) collective-permute-start(f32[16,128]{1,0:T(8,128)S(1)} %pad_maximum_fusion.1), channel_id=1, source_target_pairs={{0,4},{4,0},{1,5},{5,1},{2,6},{6,2},{3,7},{7,3},{8,12},{12,8},{9,1... | collective-permute-start | bytes 24584 | tf_op jit(solution)/shard_map/ppermute | solution.py:17
  105.3 0.1 fusion.72
  105.4 1.0 collective-permute-done.2
  106.3 0.1 fusion.77
  106.4 2.7 %fusion = f32[192,1536]{1,0:T(8,128)S(1)} fusion(bf16[1024,1664]{1,0:T(8,128)(2,1)} %all-gather.2.cloned.1.call-done, f32[192,1024]{1,0:T(8,128)S(1)} %get-tuple-element.15, f32[1024]{0:T(1024)S(1)} %get-tuple-element.8, s32[1024]{0:T(1024)S(1)} %fusion.69, pred[1024]{0:T(1024)(128)(4,1)S(1)} %fusion.72), kind=kOutput, calls=%fused_computation | convolution fusion | flops 605159424 | bytes 5121024 | tf_op jit(solution)/shard_map/at,te->ae/dot_general | solution.py:90
  109.1 5.2 %collective-permute-start.3 = (bf16[96,1536]{1,0:T(8,128)(2,1)S(1)}, bf16[96,1536]{1,0:T(8,128)(2,1)S(1)}, u32[]{:S(2)}, u32[]{:S(2)}) collective-permute-start(bf16[96,1536]{1,0:T(8,128)(2,1)S(1)} %slice.111), channel_id=1, source_target_pairs={{0,8},{8,0},{1,9},{9,1},{2,10},{10,2},{3,11},{11,3},{4,12},{12,4},... | collective-permute-start | bytes 884744 | tf_op jit(solution)/shard_map/ppermute | solution.py:17
  114.4 1.2 collective-permute-done.3
  115.6 0.8 fusion.9
  116.3 7.6 %all-to-all-start.3 = ((bf16[6,16,1536]{2,1,0:T(8,128)(2,1)}), bf16[6,16,1536]{2,1,0:T(8,128)(2,1)S(1)}, u32[]{:S(2)}, u32[]{:S(2)}) async-start(bf16[6,16,1536]{2,1,0:T(8,128)(2,1)} %bitcast.17), calls=%async_computation.3 | async-start | bytes 589824 | tf_op jit(solution)/shard_map/all_to_all | solution.py:92
  124.0 0.6 dynamic-slice_bitcast_fusion
  124.5 13.4 %all-to-all-done.3 = bf16[6,16,1536]{2,1,0:T(8,128)(2,1)S(1)} async-done(((bf16[6,16,1536]{2,1,0:T(8,128)(2,1)}), bf16[6,16,1536]{2,1,0:T(8,128)(2,1)S(1)}, u32[]{:S(2)}, u32[]{:S(2)}) %all-to-all-start.3) | async-done | bytes 294944 | tf_op jit(solution)/shard_map/all_to_all | solution.py:92
  138.0 0.7 broadcast_multiply_fusion
  (19 shorter events, 0.3 us)
Async XLA Ops:
  7.2 4.0 %copy-start = (bf16[4096,192]{0,1:T(8,128)(2,1)S(1)}, bf16[4096,192]{0,1:T(8,128)(2,1)}, u32[]{:S(2)}) copy-start(bf16[4096,192]{0,1:T(8,128)(2,1)} %param.8) | copy-start | bytes 4718596
  7.2 4.0 %copy-start.2 = (bf16[128,4096]{1,0:T(8,128)(2,1)S(1)}, bf16[128,4096]{1,0:T(8,128)(2,1)}, u32[]{:S(2)}) copy-start(bf16[128,4096]{1,0:T(8,128)(2,1)} %param.7) | copy-start | bytes 3145732
  7.2 64.2 %all-gather.2.cloned.1.call-start = ((), (), s32[]{:S(2)}) async-start(), calls=%async_computation.4 | async-start | bytes 3833856 | tf_op jit(solution)/shard_map/all_gather | solution.py:41
  14.3 11.1 %all-to-all-start = ((bf16[4,2,16,1536]{3,2,1,0:T(8,128)(2,1)}), bf16[4,2,16,1536]{3,2,1,0:T(8,128)(2,1)S(1)}, u32[]{:S(2)}, u32[]{:S(2)}) async-start(bf16[4,2,16,1536]{3,2,1,0:T(8,128)(2,1)} %bitcast.34), calls=%async_computation | async-start | bytes 786432 | tf_op jit(solution)/shard_map/all_to_all | solution.py:47
  25.4 17.0 %collective-permute-start = (bf16[16,1536]{1,0:T(8,128)(2,1)S(1)}, bf16[16,1536]{1,0:T(8,128)(2,1)S(1)}, u32[]{:S(2)}, u32[]{:S(2)}) collective-permute-start(bf16[16,1536]{1,0:T(8,128)(2,1)S(1)} %fusion.28), channel_id=1, source_target_pairs={{0,4},{4,0},{1,5},{5,1},{2,6},{6,2},{3,7},{7,3},{8,12},{12,8},{9,1... | collective-permute-start | bytes 147464 | tf_op jit(solution)/shard_map/ppermute | solution.py:17
  43.4 18.0 %all-to-all-start.1 = ((bf16[6,16,1536]{2,1,0:T(8,128)(2,1)}), bf16[6,16,1536]{2,1,0:T(8,128)(2,1)S(1)}, u32[]{:S(2)}, u32[]{:S(2)}) async-start(bf16[6,16,1536]{2,1,0:T(8,128)(2,1)} %broadcast_in_dim.29), calls=%async_computation.1 | async-start | bytes 589824 | tf_op jit(solution)/shard_map/all_to_all | solution.py:22
  61.5 11.0 %collective-permute-start.1 = (bf16[96,1536]{1,0:T(8,128)(2,1)S(1)}, bf16[96,1536]{1,0:T(8,128)(2,1)S(1)}, u32[]{:S(2)}, u32[]{:S(2)}) collective-permute-start(bf16[96,1536]{1,0:T(8,128)(2,1)S(1)} %bitcast.36), channel_id=1, source_target_pairs={{0,8},{8,0},{1,9},{9,1},{2,10},{10,2},{3,11},{11,3},{4,12},{12,4},... | collective-permute-start | bytes 884744 | tf_op jit(solution)/shard_map/ppermute | solution.py:17
  75.5 8.0 %copy-start.1 = (s32[96]{0:T(128)S(1)}, s32[96]{0:T(128)}, u32[]{:S(2)}) copy-start(s32[96]{0:T(128)} %param.13) | copy-start | bytes 1156
  76.5 18.2 %all-to-all-start.2 = ((f32[32,16,128]{2,1,0:T(8,128)}), f32[32,16,128]{2,1,0:T(8,128)S(1)}, u32[]{:S(2)}, u32[]{:S(2)}) async-start(f32[32,16,128]{2,1,0:T(8,128)} %broadcast_in_dim.35), calls=%async_computation.2 | async-start | bytes 524288 | tf_op jit(solution)/shard_map/all_to_all | solution.py:22
  94.8 11.5 %collective-permute-start.2 = (f32[16,128]{1,0:T(8,128)S(1)}, f32[16,128]{1,0:T(8,128)S(1)}, u32[]{:S(2)}, u32[]{:S(2)}) collective-permute-start(f32[16,128]{1,0:T(8,128)S(1)} %pad_maximum_fusion.1), channel_id=1, source_target_pairs={{0,4},{4,0},{1,5},{5,1},{2,6},{6,2},{3,7},{7,3},{8,12},{12,8},{9,1... | collective-permute-start | bytes 24584 | tf_op jit(solution)/shard_map/ppermute | solution.py:17
  109.1 6.4 %collective-permute-start.3 = (bf16[96,1536]{1,0:T(8,128)(2,1)S(1)}, bf16[96,1536]{1,0:T(8,128)(2,1)S(1)}, u32[]{:S(2)}, u32[]{:S(2)}) collective-permute-start(bf16[96,1536]{1,0:T(8,128)(2,1)S(1)} %slice.111), channel_id=1, source_target_pairs={{0,8},{8,0},{1,9},{9,1},{2,10},{10,2},{3,11},{11,3},{4,12},{12,4},... | collective-permute-start | bytes 884744 | tf_op jit(solution)/shard_map/ppermute | solution.py:17
  116.3 21.6 %all-to-all-start.3 = ((bf16[6,16,1536]{2,1,0:T(8,128)(2,1)}), bf16[6,16,1536]{2,1,0:T(8,128)(2,1)S(1)}, u32[]{:S(2)}, u32[]{:S(2)}) async-start(bf16[6,16,1536]{2,1,0:T(8,128)(2,1)} %bitcast.17), calls=%async_computation.3 | async-start | bytes 589824 | tf_op jit(solution)/shard_map/all_to_all | solution.py:92
Sparse Core Ops, SparseCore 0:
  11.3 60.0 all-gather.1

commit v2 on v1

--- a/solution.py
+++ b/solution.py
@@ -35,10 +35,8 @@
     scale = jnp.exp(log_scale)
 
     text_unit = unit_rows(text_embed.astype(F32)).astype(BF16)
-    low = jnp.broadcast_to((pair_index % rows).astype(BF16)[None], (rows // 2, rows))
-    high = jnp.broadcast_to((pair_index // rows).astype(BF16)[None], (rows // 2, rows))
-    packed = jnp.concatenate([text_unit, jnp.concatenate([low, high], 0)], axis=1)
-    text_all = lax.all_gather(packed, "y", axis=0, tiled=True)
+    text = lax.all_gather(text_unit, "y", axis=0, tiled=True)
+    pairs = spread(pair_index[None], "y", n_y).reshape(1, n_y * rows)
 
     pre_act = jnp.dot(audio_hidden, head_in, preferred_element_type=F32)
     hidden = jax.nn.gelu(pre_act, approximate=False).astype(BF16)
@@ -55,40 +53,39 @@
     audio = jnp.concatenate([own, swapped(own, "c")], axis=0)
     half = n_zl * share
 
-    text = text_all[:, :width]
-    extra = text_all[:, width:].reshape(n_y, rows, rows)
-    low = extra[:, 0].astype(jnp.int32)
-    high = extra[:, rows // 2].astype(jnp.int32)
+    low = pairs % rows
+    high = pairs // rows
     pair_c = high % 2
     pair_y = (high // 2) % n_y
     pair_zl = high // (2 * n_y)
     held = (pair_y == y) & (low // share == zh * n_x + x)
     column = jnp.where(pair_c == c, 0, half) + pair_zl * share + low % share
-    column = jnp.where(held, column, -1).reshape(1, n_y * rows)
+    column = jnp.where(held, column, -1)
     onehot = lax.broadcasted_iota(jnp.int32, (2 * half, n_y * rows), 0) == column
 
     logits = scale * jnp.einsum("ae,te->at", audio, text, preferred_element_type=F32)
     local = log_sum_exp(logits, 0).reshape(n_y, rows)
-    picked = jnp.sum(jnp.where(onehot, logits, 0.0), axis=0).reshape(n_y, rows)
-
-    stats = spread(jnp.concatenate([local, picked], 0), ("y", "x"), n_y * n_x)
-    local = log_sum_exp(stats[:, :n_y], 0)
-    picked = jnp.sum(stats[:, n_y:], axis=0)
-    both = swapped(jnp.concatenate([local, picked], 0), "zh")
-    total = log_sum_exp(jnp.stack([local, both[:n_y]]), 0)
-    picked = picked + both[n_y:]
+    group = ("y", "zh", "x")
+    total = log_sum_exp(spread(local, group, n_y * n_zh * n_x), 0)
+    picked = jnp.sum(jnp.where(onehot, logits, 0.0), axis=0).reshape(-1, 1, share)
+    picked = jnp.sum(lax.all_to_all(picked, group, 0, 0), axis=0)[0]
 
     counts = lax.dynamic_slice_in_dim(valid_count.reshape(n_zl, n_y, 2), zl, 1, 0)[0]
     counts = jnp.where(c == 0, counts[:, 0], counts[:, 1])
     valid = lax.broadcasted_iota(jnp.int32, (n_y, rows), 1) < counts[:, None]
-    losses = jnp.where(valid, total - picked, 0.0)
-    losses = lax.dynamic_index_in_dim(losses, y, 0, False)
-    row_loss = lax.dynamic_slice_in_dim(losses, (zh * n_x + x) * share, share, 0)
+    first = (zh * n_x + x) * share
+    own_total = lax.dynamic_index_in_dim(total, y, 0, False)
+    own_total = lax.dynamic_slice_in_dim(own_total, first, share, 0)
+    own_count = lax.dynamic_index_in_dim(counts, y, 0, False)
+    own_valid = first + jnp.arange(share, dtype=jnp.int32) < own_count
+    row_loss = jnp.where(own_valid, own_total - picked, 0.0)
 
     weights = jnp.exp(logits - total.reshape(1, -1)) - onehot.astype(F32)
     weights = jnp.where(valid.reshape(1, -1), weights, 0.0).astype(BF16)
-    terms = jnp.einsum("at,te->ae", weights, text, preferred_element_type=F32)
-    kept = terms[:half] + swapped(terms[half:].astype(BF16), "c").astype(F32)
+    sent = jnp.einsum("at,te->ae", weights[half:], text, preferred_element_type=F32)
+    sent = swapped(sent.astype(BF16), "c")
+    kept = jnp.einsum("at,te->ae", weights[:half], text, preferred_element_type=F32)
+    kept = kept + sent.astype(F32)
     parts = lax.all_to_all(kept.astype(BF16).reshape(n_zl, share, width), "zl", 0, 0)
     grad_audio = scale * jnp.sum(parts.astype(F32), axis=0)
     return (row_loss, grad_audio)

time: 146 us -> 169 us (1.16)
  blocking collectives: 0 us -> 17.8 us
  waiting for transfers between devices: 48.2 us -> 54.1 us
  starting transfers between devices: 64 us -> 60.5 us
  matrix products: 8.06 us -> 11.5 us
    all_to_all x0 -> x1, blocking collectives: none -> 17.8 us  [spread(): return lax.all_to_all(chunks, axis, 0, 0)]
    all_to_all x0 -> x1, waiting for transfers between devices: none -> 12.2 us  [on_device(): picked = jnp.sum(lax.all_to_all(picked, group, 0, 0), axis=0)[0]]
    ppermute x4 -> x3, starting transfers between devices: 37.6 us -> 26.7 us  [swapped(): return lax.ppermute(value, axis, [(0, 1), (1, 0)])]
    all_to_all x0 -> x1, starting transfers between devices: none -> 7.98 us  [on_device(): picked = jnp.sum(lax.all_to_all(picked, group, 0, 0), axis=0)[0]]
    all_to_all x1, starting transfers between devices: 7.63 us -> 3.43 us  [on_device(): lax.all_to_all(kept.astype(BF16).reshape(n_zl, share, width), 'zl', 0, 0)]
    all_to_all x2, starting transfers between devices: 13.9 us -> 17.5 us  [spread(): return lax.all_to_all(chunks, axis, 0, 0)]
    all_gather x1, waiting for transfers between devices: 3.51 us -> 0.02 us  [on_device(): text = lax.all_gather(text_unit, 'y', axis=0, tiled=True)]
    dot_general x1 -> x2, matrix products: 2.69 us -> 5.77 us  [the longest x1 3.25 us: on_device(): jnp.einsum('at,te->ae', weights[:half], text, preferred_element_type=F32)]
  transfers between devices with their start and end apart: 9 -> 9, of which waited for: 8 -> 6; matrix products, arithmetic and copies ran while one was open for 4% -> 6% of each run, Pallas kernels for 0% -> 0%
where the time goes in v2:
time: 169 us
  starting transfers between devices  60.5 us (36%)
  waiting for transfers between devices  54.1 us (32%)
  blocking collectives  17.8 us (11%)
  between operations  15 us (9%)
  matrix products  11.5 us (7%)
  other arithmetic  6.13 us (4%)
  local copies, waits for them, and re-layouts  3.62 us (2%)
    ppermute x3, starting transfers between devices, swapped(): return lax.ppermute(value, axis, [(0, 1), (1, 0)])  26.7 us
    all_to_all x2, waiting for transfers between devices, spread(): return lax.all_to_all(chunks, axis, 0, 0)  22.2 us
    all_to_all x1, blocking collectives, spread(): return lax.all_to_all(chunks, axis, 0, 0)  17.8 us
    all_to_all x2, starting transfers between devices, spread(): return lax.all_to_all(chunks, axis, 0, 0)  17.5 us
    all_to_all x1, waiting for transfers between devices, on_device(): picked = jnp.sum(lax.all_to_all(picked, group, 0, 0), axis=0)[0]  12.2 us
    all_to_all x1, waiting for transfers between devices, on_device(): lax.all_to_all(kept.astype(BF16).reshape(n_zl, share, width), 'zl', 0, 0)  11.9 us
    all_to_all x1, starting transfers between devices, on_device(): picked = jnp.sum(lax.all_to_all(picked, group, 0, 0), axis=0)[0]  7.98 us
    all_to_all x1, waiting for transfers between devices, on_device(): partial = lax.all_to_all(partial, 'x', 0, 0)  6.23 us
  transfers between devices with their start and end apart: 9, of which 6 were waited for; matrix products, arithmetic and copies ran while one was open for 6% of the time, Pallas kernels for 0%

profile of v2, /device:TPU:1, one launch (start us, length us, event | category | flops | bytes accessed | tf_op | source)
XLA Modules:
  0.0 168.6 jit_solution(6131806051846797586)
XLA Ops:
  7.2 0.0 copy-start
  7.2 0.0 all-gather.2.cloned.1.call-start
  7.2 1.3 fusion
  8.5 1.9 %fusion.1 = bf16[128,1536]{1,0:T(8,128)(2,1)} fusion(bf16[128,1536]{1,0:T(8,128)(2,1)} %param.10, f32[128]{0:T(128)S(1)} %add_rsqrt_fusion), kind=kLoop, calls=%fused_computation.6 | loop fusion | flops 589824 | bytes 786944 | tf_op jit(solution)/shard_map/convert_element_type | solution.py:37
  10.4 0.0 all-gather.2.cloned.1.call-update
  10.4 0.0 copy-done
  10.4 0.0 copy-start.1
  10.4 2.6 %convolution_convert_fusion = bf16[128,1536]{1,0:T(8,128)(2,1)S(1)} fusion(bf16[192,1536]{1,0:T(8,128)(2,1)} %param.9, bf16[128,4096]{1,0:T(8,128)(2,1)} %param.7, bf16[4096,192]{0,1:T(8,128)(2,1)S(1)} %copy-done), kind=kOutput, calls=%fused_computation | convolution fusion | flops 278618112 | bytes 3604480 | tf_op jit(solution)/shard_map/dot_general | solution.py:43
  13.0 0.8 copy.18
  13.8 4.8 %all-to-all-start = ((bf16[4,2,16,1536]{3,2,1,0:T(8,128)(2,1)}), bf16[4,2,16,1536]{3,2,1,0:T(8,128)(2,1)S(1)}, u32[]{:S(2)}, u32[]{:S(2)}) async-start(bf16[4,2,16,1536]{3,2,1,0:T(8,128)(2,1)} %bitcast.34), calls=%async_computation | async-start | bytes 786432 | tf_op jit(solution)/shard_map/all_to_all | solution.py:45
  18.6 6.2 %all-to-all-done = bf16[4,2,16,1536]{3,2,1,0:T(8,128)(2,1)S(1)} async-done(((bf16[4,2,16,1536]{3,2,1,0:T(8,128)(2,1)}), bf16[4,2,16,1536]{3,2,1,0:T(8,128)(2,1)S(1)}, u32[]{:S(2)}, u32[]{:S(2)}) %all-to-all-start) | async-done | bytes 393248 | tf_op jit(solution)/shard_map/all_to_all | solution.py:45
  24.9 0.1 convert_reduce_fusion
  25.0 15.5 %collective-permute-start = (bf16[16,1536]{1,0:T(8,128)(2,1)S(1)}, bf16[16,1536]{1,0:T(8,128)(2,1)S(1)}, u32[]{:S(2)}, u32[]{:S(2)}) collective-permute-start(bf16[16,1536]{1,0:T(8,128)(2,1)S(1)} %fusion.21), channel_id=1, source_target_pairs={{0,4},{4,0},{1,5},{5,1},{2,6},{6,2},{3,7},{7,3},{8,12},{12,8},{9,1... | collective-permute-start | bytes 147464 | tf_op jit(solution)/shard_map/ppermute | solution.py:17
  40.5 1.5 collective-permute-done
  42.0 0.1 multiply_reduce_fusion
  42.1 0.1 multiply_convert_fusion
  42.2 17.8 %all_to_all.30 = bf16[6,16,1536]{2,1,0:T(8,128)(2,1)S(1)} all-to-all(bf16[6,16,1536]{2,1,0:T(8,128)(2,1)S(1)} %broadcast_in_dim.28), channel_id=1, replica_groups=mesh['zl'=6,'y'=8,'c'=2,'zh'=2,'x'=4] {'zl'}, dimensions={0} | all-to-all | bytes 589824 | tf_op jit(solution)/shard_map/all_to_all | solution.py:22
  60.1 6.4 %collective-permute-start.1 = (bf16[96,1536]{1,0:T(8,128)(2,1)S(1)}, bf16[96,1536]{1,0:T(8,128)(2,1)S(1)}, u32[]{:S(2)}, u32[]{:S(2)}) collective-permute-start(bf16[96,1536]{1,0:T(8,128)(2,1)S(1)} %bitcast.36), channel_id=1, source_target_pairs={{0,8},{8,0},{1,9},{9,1},{2,10},{10,2},{3,11},{11,3},{4,12},{12,4},... | collective-permute-start | bytes 884744 | tf_op jit(solution)/shard_map/ppermute | solution.py:17
  66.5 0.6 broadcast_in_dim.49
  67.1 6.8 %all-to-all-start.3 = ((s32[8,1,128]{2,1,0:T(1,128)}), s32[8,1,128]{2,1,0:T(1,128)S(1)}, u32[]{:S(2)}, u32[]{:S(2)}) async-start(s32[8,1,128]{2,1,0:T(1,128)} %broadcast_in_dim.49), calls=%async_computation.3 | async-start | bytes 8192 | tf_op jit(solution)/shard_map/all_to_all | solution.py:22
  74.6 5.8 %all-to-all-done.3 = s32[8,1,128]{2,1,0:T(1,128)S(1)} async-done(((s32[8,1,128]{2,1,0:T(1,128)}), s32[8,1,128]{2,1,0:T(1,128)S(1)}, u32[]{:S(2)}, u32[]{:S(2)}) %all-to-all-start.3) | async-done | bytes 4128 | tf_op jit(solution)/shard_map/all_to_all | solution.py:22
  80.4 0.0 copy-start.2
  80.4 0.0 collective-permute-done.1
  80.4 0.0 all-gather.2.cloned.1.call-done
  80.4 3.1 %fusion.98 = (f32[1024]{0:T(1024)S(1)}, f32[192,1024]{1,0:T(8,128)S(1)}) fusion(bf16[1024,1536]{1,0:T(8,128)(2,1)} %all-gather.2.cloned.1.call-done, bf16[96,1536]{1,0:T(8,128)(2,1)S(1)} %collective-permute-done.1, bf16[96,1536]{1,0:T(8,128)(2,1)S(1)} %bitcast.37, f32[]{:T(128)S(6)} %exp.12), kind=kOutput, calls=%fused_computation.157 | convolution fusion | flops 605551616 | bytes 4526084 | tf_op jit(solution)/shard_map/ae,te->at/dot_general | solution.py:66
  83.5 0.2 exponential_reduce_fusion
  83.7 0.7 broadcast_in_dim.48
  84.5 10.7 %all-to-all-start.2 = ((f32[64,8,128]{2,1,0:T(8,128)}), f32[64,8,128]{2,1,0:T(8,128)S(1)}, u32[]{:S(2)}, u32[]{:S(2)}) async-start(f32[64,8,128]{2,1,0:T(8,128)} %broadcast_in_dim.48), calls=%async_computation.2 | async-start | bytes 524288 | tf_op jit(solution)/shard_map/all_to_all | solution.py:22
  95.2 0.1 reshape.341
  95.4 0.1 copy.14
  95.4 0.1 fusion.63
  95.5 16.4 %all-to-all-done.2 = f32[64,8,128]{2,1,0:T(8,128)S(1)} async-done(((f32[64,8,128]{2,1,0:T(8,128)}), f32[64,8,128]{2,1,0:T(8,128)S(1)}, u32[]{:S(2)}, u32[]{:S(2)}) %all-to-all-start.2) | async-done | bytes 262176 | tf_op jit(solution)/shard_map/all_to_all | solution.py:22
  111.9 0.1 reduce_max.19
  112.0 0.1 exponential_reduce_fusion.1
  112.1 0.2 select_convert_fusion
  112.3 2.5 %convolution_convert_fusion.1 = bf16[96,1536]{1,0:T(8,128)(2,1)S(1)} fusion(bf16[1024,1536]{1,0:T(8,128)(2,1)} %all-gather.2.cloned.1.call-done, bf16[192,1024]{1,0:T(8,128)(2,1)S(1)} %select_convert_fusion), kind=kOutput, calls=%fused_computation.1 | convolution fusion | flops 302137344 | bytes 3637248 | tf_op jit(solution)/shard_map/at,te->ae/dot_general | solution.py:85
  114.8 4.8 %collective-permute-start.2 = (bf16[96,1536]{1,0:T(8,128)(2,1)S(1)}, bf16[96,1536]{1,0:T(8,128)(2,1)S(1)}, u32[]{:S(2)}, u32[]{:S(2)}) collective-permute-start(bf16[96,1536]{1,0:T(8,128)(2,1)S(1)} %convolution_convert_fusion.1), channel_id=1, source_target_pairs={{0,8},{8,0},{1,9},{9,1},{2,10},{10,2},{3,11},{11,3},{4,12},{12,4},... | collective-permute-start | bytes 884744 | tf_op jit(solution)/shard_map/ppermute | solution.py:17
  119.6 0.7 reshape.345
  120.3 8.0 %all-to-all-start.4 = ((f32[64,1,16]{2,1,0:T(1,128)}), f32[64,1,16]{2,1,0:T(1,128)S(1)}, u32[]{:S(2)}, u32[]{:S(2)}) async-start(f32[64,1,16]{2,1,0:T(1,128)} %bitcast.10), calls=%async_computation.4 | async-start | bytes 65536 | tf_op jit(solution)/shard_map/all_to_all | solution.py:71
  128.3 0.0 collective-permute-done.2
  128.3 3.2 %add_convert_fusion = bf16[96,1536]{1,0:T(8,128)(2,1)} fusion(bf16[96,1536]{1,0:T(8,128)(2,1)S(1)} %collective-permute-done.2, bf16[1024,1536]{1,0:T(8,128)(2,1)} %all-gather.2.cloned.1.call-done, bf16[192,1024]{1,0:T(8,128)(2,1)S(1)} %select_convert_fusion), kind=kOutput, calls=%fused_computation.16 | convolution fusion | flops 302432256 | bytes 3932160 | tf_op jit(solution)/shard_map/at,te->ae/dot_general | solution.py:87
  131.6 12.2 %all-to-all-done.4 = f32[64,1,16]{2,1,0:T(1,128)S(1)} async-done(((f32[64,1,16]{2,1,0:T(1,128)}), f32[64,1,16]{2,1,0:T(1,128)S(1)}, u32[]{:S(2)}, u32[]{:S(2)}) %all-to-all-start.4) | async-done | bytes 4128 | tf_op jit(solution)/shard_map/all_to_all | solution.py:71
  143.8 3.4 %all-to-all-start.5 = ((bf16[6,16,1536]{2,1,0:T(8,128)(2,1)}), bf16[6,16,1536]{2,1,0:T(8,128)(2,1)S(1)}, u32[]{:S(2)}, u32[]{:S(2)}) async-start(bf16[6,16,1536]{2,1,0:T(8,128)(2,1)} %bitcast.14), calls=%async_computation.5 | async-start | bytes 589824 | tf_op jit(solution)/shard_map/all_to_all | solution.py:89
  147.2 0.6 constant_dynamic-slice_fusion
  147.8 0.1 reduce_sum.78
  147.9 1.2 compare_select_fusion
  149.2 11.9 %all-to-all-done.5 = bf16[6,16,1536]{2,1,0:T(8,128)(2,1)S(1)} async-done(((bf16[6,16,1536]{2,1,0:T(8,128)(2,1)}), bf16[6,16,1536]{2,1,0:T(8,128)(2,1)S(1)}, u32[]{:S(2)}, u32[]{:S(2)}) %all-to-all-start.5) | async-done | bytes 294944 | tf_op jit(solution)/shard_map/all_to_all | solution.py:89
  161.1 0.7 broadcast_multiply_fusion
  (13 shorter events, 0.2 us)
Async XLA Ops:
  7.2 3.2 %copy-start = (bf16[4096,192]{0,1:T(8,128)(2,1)S(1)}, bf16[4096,192]{0,1:T(8,128)(2,1)}, u32[]{:S(2)}) copy-start(bf16[4096,192]{0,1:T(8,128)(2,1)} %param.8) | copy-start | bytes 4718596
  7.2 73.2 %all-gather.2.cloned.1.call-start = ((), (), s32[]{:S(2)}) async-start(), calls=%async_computation.6 | async-start | bytes 3538944 | tf_op jit(solution)/shard_map/all_gather | solution.py:38
  10.4 56.1 %copy-start.1 = (s32[128]{0:T(128)S(1)}, s32[128]{0:T(128)}, u32[]{:S(2)}) copy-start(s32[128]{0:T(128)} %param.12) | copy-start | bytes 1540
  13.8 11.1 %all-to-all-start = ((bf16[4,2,16,1536]{3,2,1,0:T(8,128)(2,1)}), bf16[4,2,16,1536]{3,2,1,0:T(8,128)(2,1)S(1)}, u32[]{:S(2)}, u32[]{:S(2)}) async-start(bf16[4,2,16,1536]{3,2,1,0:T(8,128)(2,1)} %bitcast.34), calls=%async_computation | async-start | bytes 786432 | tf_op jit(solution)/shard_map/all_to_all | solution.py:45
  25.0 17.0 %collective-permute-start = (bf16[16,1536]{1,0:T(8,128)(2,1)S(1)}, bf16[16,1536]{1,0:T(8,128)(2,1)S(1)}, u32[]{:S(2)}, u32[]{:S(2)}) collective-permute-start(bf16[16,1536]{1,0:T(8,128)(2,1)S(1)} %fusion.21), channel_id=1, source_target_pairs={{0,4},{4,0},{1,5},{5,1},{2,6},{6,2},{3,7},{7,3},{8,12},{12,8},{9,1... | collective-permute-start | bytes 147464 | tf_op jit(solution)/shard_map/ppermute | solution.py:17
  60.1 20.3 %collective-permute-start.1 = (bf16[96,1536]{1,0:T(8,128)(2,1)S(1)}, bf16[96,1536]{1,0:T(8,128)(2,1)S(1)}, u32[]{:S(2)}, u32[]{:S(2)}) collective-permute-start(bf16[96,1536]{1,0:T(8,128)(2,1)S(1)} %bitcast.36), channel_id=1, source_target_pairs={{0,8},{8,0},{1,9},{9,1},{2,10},{10,2},{3,11},{11,3},{4,12},{12,4},... | collective-permute-start | bytes 884744 | tf_op jit(solution)/shard_map/ppermute | solution.py:17
  67.1 13.3 %all-to-all-start.3 = ((s32[8,1,128]{2,1,0:T(1,128)}), s32[8,1,128]{2,1,0:T(1,128)S(1)}, u32[]{:S(2)}, u32[]{:S(2)}) async-start(s32[8,1,128]{2,1,0:T(1,128)} %broadcast_in_dim.49), calls=%async_computation.3 | async-start | bytes 8192 | tf_op jit(solution)/shard_map/all_to_all | solution.py:22
  80.4 14.8 %copy-start.2 = (s32[96]{0:T(128)S(1)}, s32[96]{0:T(128)}, u32[]{:S(2)}) copy-start(s32[96]{0:T(128)} %param.13) | copy-start | bytes 1156
  84.5 27.5 %all-to-all-start.2 = ((f32[64,8,128]{2,1,0:T(8,128)}), f32[64,8,128]{2,1,0:T(8,128)S(1)}, u32[]{:S(2)}, u32[]{:S(2)}) async-start(f32[64,8,128]{2,1,0:T(8,128)} %broadcast_in_dim.48), calls=%async_computation.2 | async-start | bytes 524288 | tf_op jit(solution)/shard_map/all_to_all | solution.py:22
  114.8 13.5 %collective-permute-start.2 = (bf16[96,1536]{1,0:T(8,128)(2,1)S(1)}, bf16[96,1536]{1,0:T(8,128)(2,1)S(1)}, u32[]{:S(2)}, u32[]{:S(2)}) collective-permute-start(bf16[96,1536]{1,0:T(8,128)(2,1)S(1)} %convolution_convert_fusion.1), channel_id=1, source_target_pairs={{0,8},{8,0},{1,9},{9,1},{2,10},{10,2},{3,11},{11,3},{4,12},{12,4},... | collective-permute-start | bytes 884744 | tf_op jit(solution)/shard_map/ppermute | solution.py:17
  120.3 23.5 %all-to-all-start.4 = ((f32[64,1,16]{2,1,0:T(1,128)}), f32[64,1,16]{2,1,0:T(1,128)S(1)}, u32[]{:S(2)}, u32[]{:S(2)}) async-start(f32[64,1,16]{2,1,0:T(1,128)} %bitcast.10), calls=%async_computation.4 | async-start | bytes 65536 | tf_op jit(solution)/shard_map/all_to_all | solution.py:71
  143.8 17.3 %all-to-all-start.5 = ((bf16[6,16,1536]{2,1,0:T(8,128)(2,1)}), bf16[6,16,1536]{2,1,0:T(8,128)(2,1)S(1)}, u32[]{:S(2)}, u32[]{:S(2)}) async-start(bf16[6,16,1536]{2,1,0:T(8,128)(2,1)} %bitcast.14), calls=%async_computation.5 | async-start | bytes 589824 | tf_op jit(solution)/shard_map/all_to_all | solution.py:89
Sparse Core Ops, SparseCore 0:
  10.5 57.1 all-gather.1

commit v3 on v1

--- a/solution.py
+++ b/solution.py
@@ -48,10 +48,11 @@
     halves = jnp.sum(partial.astype(F32), axis=0)
     mine = jnp.where(zh == 0, halves[0], halves[1])
     other = jnp.where(zh == 0, halves[1], halves[0])
-    raw = mine + swapped(other.astype(BF16), "zh").astype(F32)
-    audio_unit = unit_rows(raw).astype(BF16)
+    halves = jnp.concatenate([mine, other], axis=0)
+    crossed = swapped(jnp.concatenate([other, mine], axis=0).astype(BF16), "zh")
+    audio_unit = unit_rows(halves + crossed.astype(F32)).astype(BF16)
 
-    own = spread(audio_unit, "zl", n_zl).reshape(n_zl * share, width)
+    own = spread(audio_unit, "zl", n_zl).reshape(2 * n_zl * share, width)
     audio = jnp.concatenate([own, swapped(own, "c")], axis=0)
     half = n_zl * share
 
@@ -62,30 +63,37 @@
     pair_c = high % 2
     pair_y = (high // 2) % n_y
     pair_zl = high // (2 * n_y)
-    held = (pair_y == y) & (low // share == zh * n_x + x)
-    column = jnp.where(pair_c == c, 0, half) + pair_zl * share + low % share
-    column = jnp.where(held, column, -1).reshape(1, n_y * rows)
-    onehot = lax.broadcasted_iota(jnp.int32, (2 * half, n_y * rows), 0) == column
+    pair_t = low // share
+    held = (pair_y == y) & (pair_t % n_x == x)
+    near = pair_t // n_x == zh
+    column = jnp.where(pair_c == c, 0, 2 * half) + pair_zl * 2 * share + low % share
+    column = jnp.where(held, column + jnp.where(near, 0, share), -1).reshape(1, n_y * rows)
+    onehot = lax.broadcasted_iota(jnp.int32, (4 * half, n_y * rows), 0) == column
 
     logits = scale * jnp.einsum("ae,te->at", audio, text, preferred_element_type=F32)
-    local = log_sum_exp(logits, 0).reshape(n_y, rows)
-    picked = jnp.sum(jnp.where(onehot, logits, 0.0), axis=0).reshape(n_y, rows)
-
-    stats = spread(jnp.concatenate([local, picked], 0), ("y", "x"), n_y * n_x)
-    local = log_sum_exp(stats[:, :n_y], 0)
-    picked = jnp.sum(stats[:, n_y:], axis=0)
-    both = swapped(jnp.concatenate([local, picked], 0), "zh")
-    total = log_sum_exp(jnp.stack([local, both[:n_y]]), 0)
-    picked = picked + both[n_y:]
+    local = log_sum_exp(logits, 0).reshape(1, 1, n_y * rows)
+    picked = jnp.sum(jnp.where(onehot, logits, 0.0), axis=0).reshape(n_y, n_zh, n_x, share)
+    picked = jnp.where(zh == 0, picked[:, 0], picked[:, 1]).reshape(n_y * n_x, 1, share)
+    picked = jnp.pad(picked, ((0, 0), (0, 0), (0, rows - share)))
+    chunks = jnp.broadcast_to(local, (n_y * n_x, 1, n_y * rows))
+    stats = lax.all_to_all(jnp.concatenate([chunks, picked], 2), ("y", "x"), 0, 0)
+    total = log_sum_exp(stats[:, 0, : n_y * rows], 0).reshape(n_y, rows)
+    picked = jnp.sum(stats[:, 0, n_y * rows : n_y * rows + share], axis=0)
 
     counts = lax.dynamic_slice_in_dim(valid_count.reshape(n_zl, n_y, 2), zl, 1, 0)[0]
     counts = jnp.where(c == 0, counts[:, 0], counts[:, 1])
     valid = lax.broadcasted_iota(jnp.int32, (n_y, rows), 1) < counts[:, None]
-    losses = jnp.where(valid, total - picked, 0.0)
-    losses = lax.dynamic_index_in_dim(losses, y, 0, False)
-    row_loss = lax.dynamic_slice_in_dim(losses, (zh * n_x + x) * share, share, 0)
+    first = (zh * n_x + x) * share
+    own_total = lax.dynamic_index_in_dim(total, y, 0, False)
+    own_total = lax.dynamic_slice_in_dim(own_total, first, share, 0)
+    own_count = lax.dynamic_index_in_dim(counts, y, 0, False)
+    own_valid = first + jnp.arange(share, dtype=jnp.int32) < own_count
+    row_loss = jnp.where(own_valid, own_total - picked, 0.0)
 
-    weights = jnp.exp(logits - total.reshape(1, -1)) - onehot.astype(F32)
+    def kept_rows(values):
+        return values.reshape(2 * n_zl, 2, share, -1)[:, 0].reshape(2 * half, -1)
+
+    weights = jnp.exp(kept_rows(logits) - total.reshape(1, -1)) - kept_rows(onehot).astype(F32)
     weights = jnp.where(valid.reshape(1, -1), weights, 0.0).astype(BF16)
     terms = jnp.einsum("at,te->ae", weights, text, preferred_element_type=F32)
     kept = terms[:half] + swapped(terms[half:].astype(BF16), "c").astype(F32)

time: 146 us -> 140 us (0.959)
  starting transfers between devices: 64 us -> 50.2 us
  waiting for transfers between devices: 48.2 us -> 52.1 us
  other arithmetic: 6.16 us -> 8 us
    ppermute x4 -> x3, starting transfers between devices: 37.6 us -> 23.2 us  [swapped(): return lax.ppermute(value, axis, [(0, 1), (1, 0)])]
    all_to_all x0 -> x1, starting transfers between devices: none -> 8.88 us  [on_device(): lax.all_to_all(jnp.concatenate([chunks, picked], 2), ('y', 'x'), 0, 0)]
    all_to_all x0 -> x1, waiting for transfers between devices: none -> 8.49 us  [on_device(): lax.all_to_all(jnp.concatenate([chunks, picked], 2), ('y', 'x'), 0, 0)]
    all_to_all x1, starting transfers between devices: 7.63 us -> 3.43 us  [on_device(): lax.all_to_all(kept.astype(BF16).reshape(n_zl, share, width), 'zl', 0, 0)]
    all_to_all x2 -> x1, starting transfers between devices: 13.9 us -> 9.84 us  [spread(): return lax.all_to_all(chunks, axis, 0, 0)]
    all_gather x1, waiting for transfers between devices: 3.51 us -> 0.01 us  [on_device(): text_all = lax.all_gather(packed, 'y', axis=0, tiled=True)]
    ppermute x4 -> x3, waiting for transfers between devices: 3.64 us -> 4 us  [swapped(): return lax.ppermute(value, axis, [(0, 1), (1, 0)])]
    all_to_all x2 -> x1, waiting for transfers between devices: 21.4 us -> 21.4 us  [spread(): return lax.all_to_all(chunks, axis, 0, 0)]
  transfers between devices with their start and end apart: 9 -> 8, of which waited for: 8 -> 7; matrix products, arithmetic and copies ran while one was open for 4% -> 6% of each run, Pallas kernels for 0% -> 0%
where the time goes in v3:
time: 140 us; the launch traced here: 139 us
  waiting for transfers between devices  52.1 us (37%)
  starting transfers between devices  50.2 us (36%)
  between operations  15 us (11%)
  matrix products  8.66 us (6%)
  other arithmetic  8 us (6%)
  local copies, waits for them, and re-layouts  5.32 us (4%)
    ppermute x3, starting transfers between devices, swapped(): return lax.ppermute(value, axis, [(0, 1), (1, 0)])  23.2 us
    all_to_all x1, waiting for transfers between devices, spread(): return lax.all_to_all(chunks, axis, 0, 0)  21.4 us
    all_to_all x1, waiting for transfers between devices, on_device(): lax.all_to_all(kept.astype(BF16).reshape(n_zl, share, width), 'zl', 0, 0)  12 us
    all_to_all x1, starting transfers between devices, spread(): return lax.all_to_all(chunks, axis, 0, 0)  9.84 us
    all_to_all x1, starting transfers between devices, on_device(): lax.all_to_all(jnp.concatenate([chunks, picked], 2), ('y', 'x'), 0, 0)  8.88 us
    all_to_all x1, waiting for transfers between devices, on_device(): lax.all_to_all(jnp.concatenate([chunks, picked], 2), ('y', 'x'), 0, 0)  8.49 us
    all_to_all x1, waiting for transfers between devices, on_device(): partial = lax.all_to_all(partial, 'x', 0, 0)  6.23 us
    all_to_all x1, starting transfers between devices, on_device(): partial = lax.all_to_all(partial, 'x', 0, 0)  4.84 us
  transfers between devices with their start and end apart: 8, of which 7 were waited for; matrix products, arithmetic and copies ran while one was open for 6% of the time, Pallas kernels for 0%

profile of v3, /device:TPU:1, one launch (start us, length us, event | category | flops | bytes accessed | tf_op | source)
XLA Modules:
  0.0 139.4 jit_solution(7729511457175136222)
XLA Ops:
  7.2 0.0 copy-start
  7.2 0.0 copy-start.4
  7.2 0.0 all-gather.2.cloned.1.call-start
  7.2 0.8 fusion.77
  8.1 1.2 fusion.10
  9.2 1.1 fusion.11
  10.4 0.8 maximum_maximum_fusion
  11.2 0.0 all-gather.2.cloned.1.call-update
  11.2 0.0 copy-done
  11.2 2.3 %convolution_convert_fusion = bf16[128,1536]{1,0:T(8,128)(2,1)S(1)} fusion(bf16[192,1536]{1,0:T(8,128)(2,1)} %param.9, bf16[128,4096]{1,0:T(8,128)(2,1)S(1)} %copy-done.4, bf16[4096,192]{0,1:T(8,128)(2,1)S(1)} %copy-done), kind=kOutput, calls=%fused_computation.4 | convolution fusion | flops 278618112 | bytes 3604480 | tf_op jit(solution)/shard_map/dot_general | solution.py:45
  13.5 0.8 copy.30
  14.3 4.8 %all-to-all-start = ((bf16[4,2,16,1536]{3,2,1,0:T(8,128)(2,1)}), bf16[4,2,16,1536]{3,2,1,0:T(8,128)(2,1)S(1)}, u32[]{:S(2)}, u32[]{:S(2)}) async-start(bf16[4,2,16,1536]{3,2,1,0:T(8,128)(2,1)} %bitcast.49), calls=%async_computation | async-start | bytes 786432 | tf_op jit(solution)/shard_map/all_to_all | solution.py:47
  19.1 6.2 %all-to-all-done = bf16[4,2,16,1536]{3,2,1,0:T(8,128)(2,1)S(1)} async-done(((bf16[4,2,16,1536]{3,2,1,0:T(8,128)(2,1)}), bf16[4,2,16,1536]{3,2,1,0:T(8,128)(2,1)S(1)}, u32[]{:S(2)}, u32[]{:S(2)}) %all-to-all-start) | async-done | bytes 393248 | tf_op jit(solution)/shard_map/all_to_all | solution.py:47
  25.4 0.1 convert_reduce_fusion
  25.4 0.0 copy-start.3
  25.5 15.5 %collective-permute-start = (bf16[32,1536]{1,0:T(8,128)(2,1)S(1)}, bf16[32,1536]{1,0:T(8,128)(2,1)S(1)}, u32[]{:S(2)}, u32[]{:S(2)}) collective-permute-start(bf16[32,1536]{1,0:T(8,128)(2,1)S(1)} %pad_maximum_fusion), channel_id=1, source_target_pairs={{0,4},{4,0},{1,5},{5,1},{2,6},{6,2},{3,7},{7,3},{8,12},{12,8},{9,1... | collective-permute-start | bytes 294920 | tf_op jit(solution)/shard_map/ppermute | solution.py:17
  41.0 2.2 %collective-permute-done = bf16[32,1536]{1,0:T(8,128)(2,1)S(1)} collective-permute-done((bf16[32,1536]{1,0:T(8,128)(2,1)S(1)}, bf16[32,1536]{1,0:T(8,128)(2,1)S(1)}, u32[]{:S(2)}, u32[]{:S(2)}) %collective-permute-start) | collective-permute-done | bytes 98336 | tf_op jit(solution)/shard_map/ppermute | solution.py:17
  43.2 0.1 multiply_reduce_fusion
  43.3 0.1 multiply_convert_fusion
  43.4 0.9 broadcast_in_dim.58
  44.3 9.8 %all-to-all-start.1 = ((bf16[6,32,1536]{2,1,0:T(8,128)(2,1)}), bf16[6,32,1536]{2,1,0:T(8,128)(2,1)S(1)}, u32[]{:S(2)}, u32[]{:S(2)}) async-start(bf16[6,32,1536]{2,1,0:T(8,128)(2,1)} %broadcast_in_dim.58), calls=%async_computation.1 | async-start | bytes 1179648 | tf_op jit(solution)/shard_map/all_to_all | solution.py:22
  54.8 0.1 reshape.253
  55.0 0.1 copy.20
  55.0 21.4 %all-to-all-done.1 = bf16[6,32,1536]{2,1,0:T(8,128)(2,1)S(1)} async-done(((bf16[6,32,1536]{2,1,0:T(8,128)(2,1)}), bf16[6,32,1536]{2,1,0:T(8,128)(2,1)S(1)}, u32[]{:S(2)}, u32[]{:S(2)}) %all-to-all-start.1) | async-done | bytes 589856 | tf_op jit(solution)/shard_map/all_to_all | solution.py:22
  76.4 3.7 %collective-permute-start.1 = (bf16[192,1536]{1,0:T(8,128)(2,1)S(1)}, bf16[192,1536]{1,0:T(8,128)(2,1)}, u32[]{:S(2)}, u32[]{:S(2)}) collective-permute-start(bf16[192,1536]{1,0:T(8,128)(2,1)S(1)} %bitcast.51), channel_id=1, source_target_pairs={{0,8},{8,0},{1,9},{9,1},{2,10},{10,2},{3,11},{11,3},{4,12},{12,4},... | collective-permute-start | bytes 1769480 | tf_op jit(solution)/shard_map/ppermute | solution.py:17
  80.1 0.1 fusion.72
  80.2 1.0 slice.70
  81.2 0.6 collective-permute-done.1
  81.9 3.7 %fusion.113 = (f32[1024]{0:T(1024)S(1)}, f32[384,1024]{1,0:T(8,128)S(1)}) fusion(bf16[1024,1664]{1,0:T(8,128)(2,1)} %all-gather.2.cloned.1.call-done, bf16[192,1536]{1,0:T(8,128)(2,1)} %collective-permute-done.1, bf16[192,1536]{1,0:T(8,128)(2,1)} %bitcast.52, f32[]{:T(128)S(6)} %exp.12), kind=kOutput, calls=%fused_computation.189 | convolution fusion | flops 1211104256 | bytes 5902340 | tf_op jit(solution)/shard_map/ae,te->at/dot_general | solution.py:73
  85.6 0.4 exponential_reduce_fusion
  86.0 0.1 reshape.257
  86.1 0.8 copy.22
  86.9 8.9 %all-to-all-start.2 = ((f32[32,1,1152]{2,1,0:T(1,128)}), f32[32,1,1152]{2,1,0:T(1,128)S(1)}, u32[]{:S(2)}, u32[]{:S(2)}) async-start(f32[32,1,1152]{2,1,0:T(1,128)} %copy.22), calls=%async_computation.2 | async-start | bytes 294912 | tf_op jit(solution)/shard_map/all_to_all | solution.py:79
  95.8 1.0 slice.77
  96.8 0.1 compare_convert_fusion
  96.9 8.5 %all-to-all-done.2 = f32[32,1,1152]{2,1,0:T(1,128)S(1)} async-done(((f32[32,1,1152]{2,1,0:T(1,128)}), f32[32,1,1152]{2,1,0:T(1,128)S(1)}, u32[]{:S(2)}, u32[]{:S(2)}) %all-to-all-start.2) | async-done | bytes 147488 | tf_op jit(solution)/shard_map/all_to_all | solution.py:79
  105.4 0.1 fusion.112
  105.6 0.2 fusion.13
  105.8 2.7 %fusion = f32[192,1536]{1,0:T(8,128)S(1)} fusion(bf16[192,1024]{1,0:T(8,128)(2,1)S(1)} %fusion.13, bf16[1024,1664]{1,0:T(8,128)(2,1)} %all-gather.2.cloned.1.call-done), kind=kOutput, calls=%fused_computation | convolution fusion | flops 603979776 | bytes 4718592 | tf_op jit(solution)/shard_map/at,te->ae/dot_general | solution.py:98
  108.5 4.0 %collective-permute-start.2 = (bf16[96,1536]{1,0:T(8,128)(2,1)S(1)}, bf16[96,1536]{1,0:T(8,128)(2,1)S(1)}, u32[]{:S(2)}, u32[]{:S(2)}) collective-permute-start(bf16[96,1536]{1,0:T(8,128)(2,1)S(1)} %slice.103), channel_id=1, source_target_pairs={{0,8},{8,0},{1,9},{9,1},{2,10},{10,2},{3,11},{11,3},{4,12},{12,4},... | collective-permute-start | bytes 884744 | tf_op jit(solution)/shard_map/ppermute | solution.py:17
  112.5 1.2 collective-permute-done.2
  113.7 0.8 fusion.15
  114.5 3.4 %all-to-all-start.3 = ((bf16[6,16,1536]{2,1,0:T(8,128)(2,1)}), bf16[6,16,1536]{2,1,0:T(8,128)(2,1)S(1)}, u32[]{:S(2)}, u32[]{:S(2)}) async-start(bf16[6,16,1536]{2,1,0:T(8,128)(2,1)} %bitcast.18), calls=%async_computation.3 | async-start | bytes 589824 | tf_op jit(solution)/shard_map/all_to_all | solution.py:100
  118.0 0.6 constant_dynamic-slice_fusion
  118.5 0.1 slice_reduce_fusion
  118.6 1.2 compare_select_fusion
  119.8 12.0 %all-to-all-done.3 = bf16[6,16,1536]{2,1,0:T(8,128)(2,1)S(1)} async-done(((bf16[6,16,1536]{2,1,0:T(8,128)(2,1)}), bf16[6,16,1536]{2,1,0:T(8,128)(2,1)S(1)}, u32[]{:S(2)}, u32[]{:S(2)}) %all-to-all-start.3) | async-done | bytes 294944 | tf_op jit(solution)/shard_map/all_to_all | solution.py:100
  131.9 0.7 broadcast_multiply_fusion
  (28 shorter events, 0.3 us)
Async XLA Ops:
  7.2 4.0 %copy-start = (bf16[4096,192]{0,1:T(8,128)(2,1)S(1)}, bf16[4096,192]{0,1:T(8,128)(2,1)}, u32[]{:S(2)}) copy-start(bf16[4096,192]{0,1:T(8,128)(2,1)} %param.8) | copy-start | bytes 4718596
  7.2 4.0 %copy-start.4 = (bf16[128,4096]{1,0:T(8,128)(2,1)S(1)}, bf16[128,4096]{1,0:T(8,128)(2,1)}, u32[]{:S(2)}) copy-start(bf16[128,4096]{1,0:T(8,128)(2,1)} %param.7) | copy-start | bytes 3145732
  7.2 73.0 %all-gather.2.cloned.1.call-start = ((), (), s32[]{:S(2)}) async-start(), calls=%async_computation.4 | async-start | bytes 3833856 | tf_op jit(solution)/shard_map/all_gather | solution.py:41
  14.3 11.1 %all-to-all-start = ((bf16[4,2,16,1536]{3,2,1,0:T(8,128)(2,1)}), bf16[4,2,16,1536]{3,2,1,0:T(8,128)(2,1)S(1)}, u32[]{:S(2)}, u32[]{:S(2)}) async-start(bf16[4,2,16,1536]{3,2,1,0:T(8,128)(2,1)} %bitcast.49), calls=%async_computation | async-start | bytes 786432 | tf_op jit(solution)/shard_map/all_to_all | solution.py:47
  25.4 29.4 %copy-start.3 = (s32[96]{0:T(128)S(1)}, s32[96]{0:T(128)}, u32[]{:S(2)}) copy-start(s32[96]{0:T(128)} %param.13) | copy-start | bytes 1156
  25.5 17.7 %collective-permute-start = (bf16[32,1536]{1,0:T(8,128)(2,1)S(1)}, bf16[32,1536]{1,0:T(8,128)(2,1)S(1)}, u32[]{:S(2)}, u32[]{:S(2)}) collective-permute-start(bf16[32,1536]{1,0:T(8,128)(2,1)S(1)} %pad_maximum_fusion), channel_id=1, source_target_pairs={{0,4},{4,0},{1,5},{5,1},{2,6},{6,2},{3,7},{7,3},{8,12},{12,8},{9,1... | collective-permute-start | bytes 294920 | tf_op jit(solution)/shard_map/ppermute | solution.py:17
  44.3 32.2 %all-to-all-start.1 = ((bf16[6,32,1536]{2,1,0:T(8,128)(2,1)}), bf16[6,32,1536]{2,1,0:T(8,128)(2,1)S(1)}, u32[]{:S(2)}, u32[]{:S(2)}) async-start(bf16[6,32,1536]{2,1,0:T(8,128)(2,1)} %broadcast_in_dim.58), calls=%async_computation.1 | async-start | bytes 1179648 | tf_op jit(solution)/shard_map/all_to_all | solution.py:22
  76.4 4.8 %copy-start.2 = (bf16[6,32,1536]{2,1,0:T(8,128)(2,1)}, bf16[6,32,1536]{2,1,0:T(8,128)(2,1)S(1)}, u32[]{:S(2)}) copy-start(bf16[6,32,1536]{2,1,0:T(8,128)(2,1)S(1)} %all-to-all-done.1) | copy-start | bytes 1769476
  76.4 5.4 %collective-permute-start.1 = (bf16[192,1536]{1,0:T(8,128)(2,1)S(1)}, bf16[192,1536]{1,0:T(8,128)(2,1)}, u32[]{:S(2)}, u32[]{:S(2)}) collective-permute-start(bf16[192,1536]{1,0:T(8,128)(2,1)S(1)} %bitcast.51), channel_id=1, source_target_pairs={{0,8},{8,0},{1,9},{9,1},{2,10},{10,2},{3,11},{11,3},{4,12},{12,4},... | collective-permute-start | bytes 1769480 | tf_op jit(solution)/shard_map/ppermute | solution.py:17
  86.9 18.5 %all-to-all-start.2 = ((f32[32,1,1152]{2,1,0:T(1,128)}), f32[32,1,1152]{2,1,0:T(1,128)S(1)}, u32[]{:S(2)}, u32[]{:S(2)}) async-start(f32[32,1,1152]{2,1,0:T(1,128)} %copy.22), calls=%async_computation.2 | async-start | bytes 294912 | tf_op jit(solution)/shard_map/all_to_all | solution.py:79
  96.8 8.8 %copy-start.1 = (f32[12,1,16,1024]{3,2,1,0:T(8,128)S(1)}, f32[12,1,16,1024]{3,2,1,0:T(8,128)}, u32[]{:S(2)}) copy-start(f32[12,1,16,1024]{3,2,1,0:T(8,128)} %slice.77) | copy-start | bytes 2359300
  108.5 5.2 %collective-permute-start.2 = (bf16[96,1536]{1,0:T(8,128)(2,1)S(1)}, bf16[96,1536]{1,0:T(8,128)(2,1)S(1)}, u32[]{:S(2)}, u32[]{:S(2)}) collective-permute-start(bf16[96,1536]{1,0:T(8,128)(2,1)S(1)} %slice.103), channel_id=1, source_target_pairs={{0,8},{8,0},{1,9},{9,1},{2,10},{10,2},{3,11},{11,3},{4,12},{12,4},... | collective-permute-start | bytes 884744 | tf_op jit(solution)/shard_map/ppermute | solution.py:17
  114.5 17.3 %all-to-all-start.3 = ((bf16[6,16,1536]{2,1,0:T(8,128)(2,1)}), bf16[6,16,1536]{2,1,0:T(8,128)(2,1)S(1)}, u32[]{:S(2)}, u32[]{:S(2)}) async-start(bf16[6,16,1536]{2,1,0:T(8,128)(2,1)} %bitcast.18), calls=%async_computation.3 | async-start | bytes 589824 | tf_op jit(solution)/shard_map/all_to_all | solution.py:100
Sparse Core Ops, SparseCore 0:
  11.3 60.0 all-gather.1

commit v4 on v2

v4 whole, which is shorter than its diff:
```python
import functools

import jax
import jax.numpy as jnp
from jax import lax
from jax.experimental import pallas as pl
from jax.experimental.pallas import tpu as pltpu
from jax.sharding import Mesh, PartitionSpec as P

BATCH = ("zl", "y", "c")
TENSOR = ("zh", "x")
BF16 = jnp.bfloat16
F32 = jnp.float32
I32 = jnp.int32
VMEM = pl.BlockSpec(memory_space=pltpu.VMEM)
HBM = pl.BlockSpec(memory_space=pl.ANY)
SMEM = pl.BlockSpec(memory_space=pltpu.SMEM)
LAST = (((1,), (1,)), ((), ()))
INNER = (((1,), (0,)), ((), ()))


def unit_rows(values):
    return values * lax.rsqrt(jnp.sum(values * values, axis=1, keepdims=True) + 1e-06)


def swapped(value, axis):
    return lax.ppermute(value, axis, [(0, 1), (1, 0)])


def spread(value, axis, count):
    chunks = jnp.broadcast_to(value[None], (count,) + value.shape)
    return lax.all_to_all(chunks, axis, 0, 0)


def started(sems, *pairs):
    copies = [pltpu.make_async_copy(a, b, sems.at[i]) for i, (a, b) in enumerate(pairs)]
    for copy in copies:
        copy.start()
    return copies


def pack_kernel(text_hbm, pair_hbm, out_ref, text_ref, pair_ref, sems):
    rows, width = text_ref.shape
    text_copy, pair_copy = started(sems, (text_hbm, text_ref), (pair_hbm, pair_ref))
    pair_copy.wait()
    pair = pair_ref[...]
    half = rows // 2
    low = lax.rem(pair, rows).astype(F32)
    high = lax.div(pair, rows).astype(F32)
    out_ref[:half, width:] = jnp.broadcast_to(low, (half, rows)).astype(BF16)
    out_ref[half:, width:] = jnp.broadcast_to(high, (half, rows)).astype(BF16)
    text_copy.wait()
    out_ref[:, :width] = unit_rows(text_ref[...].astype(F32)).astype(BF16)


def head_kernel(audio_hbm, first_hbm, second_hbm, out_ref, audio_ref, first_ref, second_ref, sems):
    n_x, n_zh, share, _ = out_ref.shape
    depth = audio_ref.shape[1]
    pieces = 4
    spans = [pl.ds(i * depth // pieces, depth // pieces) for i in range(pieces)]
    pairs = []
    for span in spans:
        pairs.append((audio_hbm.at[:, span], audio_ref.at[:, span]))
        pairs.append((first_hbm.at[:, span], first_ref.at[:, span]))
    copies = started(sems, *pairs, (second_hbm, second_ref))
    pre_act = 0.0
    for i, span in enumerate(spans):
        copies[2 * i].wait()
        copies[2 * i + 1].wait()
        pre_act += lax.dot_general(audio_ref[:, span], first_ref[:, span], LAST, preferred_element_type=F32)
    hidden = 0.5 * pre_act * (1.0 + lax.erf(pre_act * 0.7071067811865476))
    copies[-1].wait()
    partial = lax.dot_general(
        hidden.astype(BF16), second_ref[...], INNER, preferred_element_type=F32
    ).astype(BF16)
    for zh in range(n_zh):
        for x in range(n_x):
            start = (zh * n_x + x) * share
            out_ref[x, zh] = partial[start : start + share]


def pair_columns(text_ref, block, rows, width, place, sizes, share):
    zl, y, c, zh, x = place
    n_y, n_x = sizes
    start = block * rows
    low = text_ref[start : start + 16, width:].astype(F32)[0:1].astype(I32)
    start = start + rows // 2
    high = text_ref[start : start + 16, width:].astype(F32)[0:1].astype(I32)
    pair_t = lax.div(low, share)
    held = (lax.rem(lax.div(high, 2), n_y) == y) & (lax.rem(pair_t, n_x) == x)
    column = lax.div(high, 2 * n_y) * share + lax.rem(low, share)
    near_c = lax.rem(high, 2) == c
    return held, column, near_c, lax.div(pair_t, n_x)


def logits_kernel(place_ref, scale_ref, own_ref, other_ref, text_ref, kept_ref, stats_ref, *, sizes, share):
    n_y, n_x = sizes
    audio_rows, width = own_ref.shape
    rows = text_ref.shape[0] // n_y
    place = tuple(place_ref[i] for i in range(5))
    scale = scale_ref[0]
    n_zl = audio_rows // (2 * share)
    step = 2 * rows
    zh = place[3]
    row_ids = lax.broadcasted_iota(I32, (audio_rows, step), 0)
    for q in range(n_y // 2):
        span = slice(q * step, (q + 1) * step)
        text = text_ref[span, :width]
        parts = [pair_columns(text_ref, 2 * q + i, rows, width, place, sizes, share) for i in range(2)]
        wanted = []
        for near in (True, False):
            columns = []
            for held, column, near_c, pair_zh in parts:
                block = lax.div(column, share)
                spot = block * 2 * share + lax.rem(column, share) + pair_zh * share
                columns.append(jnp.where(held & (near_c == near), spot, -1))
            wanted.append(jnp.concatenate(columns, axis=1))
        logits = []
        picked = jnp.zeros((1, step), F32)
        for half, (ref, column) in enumerate(zip((own_ref, other_ref), wanted)):
            part = scale * lax.dot_general(ref[...], text, LAST, preferred_element_type=F32)
            logits.append(part)
            picked += jnp.sum(jnp.where(row_ids == column, part, 0.0), axis=0, keepdims=True)
            for zl in range(n_zl):
                to = (half * n_zl + zl) * share
                both = part[2 * zl * share : 2 * (zl + 1) * share]
                kept_ref[to : to + share, span] = jnp.where(zh == 0, both[:share], both[share:])
        top = functools.reduce(jnp.maximum, [jnp.max(p, axis=0, keepdims=True) for p in logits])
        mass = sum(jnp.sum(jnp.exp(p - top), axis=0, keepdims=True) for p in logits)
        local = top + jnp.log(mass)
        stats_ref[:, :, span] = jnp.broadcast_to(local[None], (n_y * n_x, 1, step))
        for i in range(2):
            first = (2 * q + i) * n_x
            block = picked[:, i * rows : (i + 1) * rows]
            stats_ref[first : first + n_x, :, n_y * rows :] = jnp.broadcast_to(block[None], (n_x, 1, rows))


def terms_kernel(place_ref, count_ref, stats_ref, kept_ref, text_ref, loss_ref, near_ref, far_ref, weight_ref, *, sizes, share):
    n_y, n_x = sizes
    audio_rows, width = kept_ref.shape[0], near_ref.shape[1]
    rows = text_ref.shape[0] // n_y
    half = audio_rows // 2
    place = tuple(place_ref[i] for i in range(5))
    zl, y, c, zh, x = place
    stats = stats_ref[:, :, : n_y * rows]
    top = jnp.max(stats, axis=0)
    total = top + jnp.log(jnp.sum(jnp.exp(stats - top[None]), axis=0))
    picked = jnp.sum(stats_ref[:, :, n_y * rows :], axis=0)
    row_ids = lax.broadcasted_iota(I32, (audio_rows, rows), 0)
    lane_ids = lax.broadcasted_iota(I32, (1, rows), 1)
    loss = jnp.zeros((1, rows), F32)
    for block in range(n_y):
        span = slice(block * rows, (block + 1) * rows)
        valid = lane_ids < count_ref[(zl * n_y + block) * 2 + c]
        loss = jnp.where(valid & (y == block), total[:, span] - picked, loss)
        held, column, near_c, pair_zh = pair_columns(text_ref, block, rows, width, place, sizes, share)
        column = jnp.where(held & (pair_zh == zh), column + jnp.where(near_c, 0, half), -1)
        weights = jnp.exp(kept_ref[:, span] - total[:, span]) - jnp.where(row_ids == column, 1.0, 0.0)
        weight_ref[:, span] = jnp.where(valid, weights, 0.0).astype(BF16)
    loss_ref[...] = loss
    step = 512 if width % 512 == 0 else width
    for start in range(0, width, step):
        span = slice(start, start + step)
        terms = lax.dot_general(weight_ref[...], text_ref[:, span], INNER, preferred_element_type=F32)
        near_ref[:, span] = terms[:half]
        far_ref[:, span] = terms[half:].astype(BF16)


def call(kernel, outs, specs, *args, vmem=32, scratch=(), flops=0, moved=0):
    return pl.pallas_call(
        kernel,
        out_shape=outs,
        in_specs=specs,
        out_specs=jax.tree.map(lambda _: VMEM, outs),
        scratch_shapes=scratch,
        compiler_params=pltpu.CompilerParams(vmem_limit_bytes=vmem * 2**20),
        cost_estimate=pl.CostEstimate(flops=flops, bytes_accessed=moved, transcendentals=0),
    )(*args)


def on_device(audio_hidden, head_in, head_out, text_embed, log_scale, pair_index, valid_count):
    rows, width = text_embed.shape
    n_zl, n_y, n_zh, n_x = (lax.axis_size(a) for a in ("zl", "y", "zh", "x"))
    place = [lax.axis_index(a) for a in BATCH + TENSOR]
    zl, y, c, zh, x = place
    place = jnp.stack(place).astype(I32)
    share = rows // (n_zh * n_x)
    sizes = (n_y, n_x)
    scale = jnp.exp(log_scale)
    out = jax.ShapeDtypeStruct

    packed = call(
        pack_kernel,
        out((rows, width + rows), BF16),
        [HBM, HBM],
        text_embed,
        pair_index.reshape(1, rows),
        vmem=62,
        scratch=[pltpu.VMEM((rows, width), BF16), pltpu.VMEM((1, rows), I32), pltpu.SemaphoreType.DMA((2,))],
        flops=4 * rows * width,
        moved=4 * rows * width,
    )
    text = lax.all_gather(packed, "y", axis=0, tiled=True)

    partial = call(
        head_kernel,
        out((n_x, n_zh, share, width), BF16),
        [HBM, HBM, HBM],
        audio_hidden,
        head_in.T,
        head_out,
        vmem=62,
        scratch=[
            pltpu.VMEM(audio_hidden.shape, BF16),
            pltpu.VMEM(head_in.shape[::-1], BF16),
            pltpu.VMEM(head_out.shape, BF16),
            pltpu.SemaphoreType.DMA((9,)),
        ],
        flops=2 * rows * head_in.shape[1] * (head_in.shape[0] + width),
        moved=2 * (audio_hidden.size + head_in.size + head_out.size),
    )
    partial = lax.all_to_all(partial, "x", 0, 0)
    halves = jnp.sum(partial.astype(F32), axis=0)
    mine = jnp.where(zh == 0, halves[0], halves[1])
    other = jnp.where(zh == 0, halves[1], halves[0])
    raw = mine + swapped(other.astype(BF16), "zh").astype(F32)
    audio_unit = unit_rows(raw).astype(BF16)

    own = spread(audio_unit, ("zl", "zh"), n_zl * n_zh).reshape(n_zl * n_zh * share, width)
    other = swapped(own, "c")
    half = n_zl * share

    kept, stats = call(
        functools.partial(logits_kernel, sizes=sizes, share=share),
        (out((2 * half, n_y * rows), F32), out((n_y * n_x, 1, (n_y + 1) * rows), F32)),
        [SMEM, SMEM, VMEM, VMEM, VMEM],
        place,
        scale.reshape(1),
        own,
        other,
        text,
        flops=8 * half * n_y * rows * width,
        moved=2 * text.size,
    )
    stats = lax.all_to_all(stats, ("y", "x"), 0, 0)
    losses, near, far = call(
        functools.partial(terms_kernel, sizes=sizes, share=share),
        (out((1, rows), F32), out((half, width), F32), out((half, width), BF16)),
        [SMEM, SMEM, VMEM, VMEM, VMEM],
        place,
        valid_count,
        stats,
        kept,
        text,
        scratch=[pltpu.VMEM((2 * half, n_y * rows), BF16)],
        flops=4 * half * n_y * rows * width,
        moved=2 * text.size,
    )
    row_loss = lax.dynamic_slice_in_dim(losses[0], (zh * n_x + x) * share, share, 0)
    near = near + swapped(far, "c").astype(F32)
    parts = lax.all_to_all(near.astype(BF16).reshape(n_zl, share, width), "zl", 0, 0)
    grad_audio = scale * jnp.sum(parts.astype(F32), axis=0)
    return (row_loss, grad_audio)


def build(mesh):
    placed = (
        P(BATCH, None),
        P(None, TENSOR),
        P(TENSOR, None),
        P(BATCH, None),
        P(),
        P(BATCH),
        P(),
    )
    return jax.shard_map(
        on_device,
        mesh=mesh,
        in_specs=placed,
        out_specs=(P(BATCH + TENSOR), P(BATCH + TENSOR, None)),
        check_vma=False,
    )


def solution(mesh):
    return build(Mesh(mesh.devices.reshape(6, 8, 2, 2, 4), BATCH + TENSOR))
```

time: 169 us -> 136 us (0.80)
  waiting for transfers between devices: 54.1 us -> 23.1 us
  blocking collectives: 17.8 us -> 47.2 us
  starting transfers between devices: 60.5 us -> 35.7 us
  matrix products: 11.5 us -> 0 us
  Pallas kernels: 0 us -> 9.99 us
  other arithmetic: 6.13 us -> 1.74 us
    all_to_all x4 -> x1, waiting for transfers between devices: 46.3 us -> 13.4 us  [on_device(): lax.all_to_all(near.astype(BF16).reshape(n_zl, share, width), 'zl', 0, 0)]
    all_to_all x4 -> x1, starting transfers between devices: 29 us -> 3.47 us  [on_device(): lax.all_to_all(near.astype(BF16).reshape(n_zl, share, width), 'zl', 0, 0)]
    all_to_all x0 -> x1, blocking collectives: none -> 17.2 us  [on_device(): stats = lax.all_to_all(stats, ('y', 'x'), 0, 0)]
    all_to_all x1, blocking collectives: 17.8 us -> 30 us  [spread(): return lax.all_to_all(chunks, axis, 0, 0)]
    dot_general x4 -> x0, matrix products: 11.5 us -> none  [the longest x1 3.25 us: on_device(): jnp.einsum('at,te->ae', weights[:half], text, preferred_element_type=F32)]
    pallas_call x0 -> x4, Pallas kernels: none -> 9.99 us  [call(): pl.pallas_call(kernel, out_shape=outs, in_specs=specs, out_specs=jax.tree...]
    ppermute x3, waiting for transfers between devices: 1.51 us -> 3.52 us  [swapped(): return lax.ppermute(value, axis, [(0, 1), (1, 0)])]
    unnamed x6, local copies, waits for them, and re-layouts: 0.02 us -> 1.97 us
  transfers between devices with their start and end apart: 9 -> 6, of which waited for: 6 -> 5; matrix products, arithmetic and copies ran while one was open for 6% -> 1% of each run, Pallas kernels for 0% -> 3%
where the time goes in v4:
time: 136 us; the launch traced here: 135 us
  blocking collectives  47.2 us (35%)
  starting transfers between devices  35.7 us (26%)
  waiting for transfers between devices  23.1 us (17%)
  between operations  14.8 us (11%)
  Pallas kernels  9.99 us (7%)
  local copies, waits for them, and re-layouts  2.68 us (2%)
  other arithmetic  1.74 us (1%)
    all_to_all x1, blocking collectives, spread(): return lax.all_to_all(chunks, axis, 0, 0)  30 us
    ppermute x3, starting transfers between devices, swapped(): return lax.ppermute(value, axis, [(0, 1), (1, 0)])  27.3 us
    all_to_all x1, blocking collectives, on_device(): stats = lax.all_to_all(stats, ('y', 'x'), 0, 0)  17.2 us
    all_to_all x1, waiting for transfers between devices, on_device(): lax.all_to_all(near.astype(BF16).reshape(n_zl, share, width), 'zl', 0, 0)  13.4 us
    pallas_call x4, Pallas kernels, call(): pl.pallas_call(kernel, out_shape=outs, in_specs=specs, out_specs=jax.tree...  9.99 us
    all_to_all x1, waiting for transfers between devices, on_device(): partial = lax.all_to_all(partial, 'x', 0, 0)  6.23 us
    all_to_all x1, starting transfers between devices, on_device(): partial = lax.all_to_all(partial, 'x', 0, 0)  4.85 us
    ppermute x3, waiting for transfers between devices, swapped(): return lax.ppermute(value, axis, [(0, 1), (1, 0)])  3.52 us
  transfers between devices with their start and end apart: 6, of which 5 were waited for; matrix products, arithmetic and copies ran while one was open for 1% of the time, Pallas kernels for 3%

profile of v4, /device:TPU:1, one launch (start us, length us, event | category | flops | bytes accessed | tf_op | source)
XLA Modules:
  0.0 135.2 jit_solution(16765483438980141309)
XLA Ops:
  7.2 0.0 all-gather.2.cloned.1.call-start
  7.2 1.9 %shard_map.87 = bf16[128,1664]{1,0:T(8,128)(2,1)} custom-call(bf16[128,1536]{1,0:T(8,128)(2,1)} %text_hbm.1, s32[1,128]{1,0:T(1,128)} %bitcast.23), custom_call_target="tpu_custom_call" | custom-call | flops 786432 | bytes 786432 | tf_op jit(solution)/shard_map/pallas_call | solution.py:170
  9.2 0.0 all-gather.2.cloned.1.call-update
  9.2 3.5 %shard_map.86 = bf16[4,2,16,1536]{3,2,1,0:T(8,128)(2,1)} custom-call(bf16[128,4096]{1,0:T(8,128)(2,1)} %audio_hbm.1, bf16[192,4096]{1,0:T(8,128)(2,1)} %bitcast.22, bf16[192,1536]{1,0:T(8,128)(2,1)} %second_hbm.1), custom_call_target="tpu_custom_call" | custom-call | flops 276824064 | bytes 3211264 | tf_op jit(solution)/shard_map/pallas_call | solution.py:170
  12.7 4.9 %all-to-all-start = ((bf16[4,2,16,1536]{3,2,1,0:T(8,128)(2,1)}), bf16[4,2,16,1536]{3,2,1,0:T(8,128)(2,1)S(1)}, u32[]{:S(2)}, u32[]{:S(2)}) async-start(bf16[4,2,16,1536]{3,2,1,0:T(8,128)(2,1)} %shard_map.86), calls=%async_computation | async-start | bytes 786432 | tf_op jit(solution)/shard_map/all_to_all | solution.py:222
  17.6 6.2 %all-to-all-done = bf16[4,2,16,1536]{3,2,1,0:T(8,128)(2,1)S(1)} async-done(((bf16[4,2,16,1536]{3,2,1,0:T(8,128)(2,1)}), bf16[4,2,16,1536]{3,2,1,0:T(8,128)(2,1)S(1)}, u32[]{:S(2)}, u32[]{:S(2)}) %all-to-all-start) | async-done | bytes 393248 | tf_op jit(solution)/shard_map/all_to_all | solution.py:222
  23.8 0.1 convert_reduce_fusion
  23.9 15.5 %collective-permute-start = (bf16[16,1536]{1,0:T(8,128)(2,1)S(1)}, bf16[16,1536]{1,0:T(8,128)(2,1)S(1)}, u32[]{:S(2)}, u32[]{:S(2)}) collective-permute-start(bf16[16,1536]{1,0:T(8,128)(2,1)S(1)} %fusion), channel_id=1, source_target_pairs={{0,4},{4,0},{1,5},{5,1},{2,6},{6,2},{3,7},{7,3},{8,12},{12,8},{9,1... | collective-permute-start | bytes 147464 | tf_op jit(solution)/shard_map/ppermute | solution.py:27
  39.4 1.5 %collective-permute-done = bf16[16,1536]{1,0:T(8,128)(2,1)S(1)} collective-permute-done((bf16[16,1536]{1,0:T(8,128)(2,1)S(1)}, bf16[16,1536]{1,0:T(8,128)(2,1)S(1)}, u32[]{:S(2)}, u32[]{:S(2)}) %collective-permute-start) | collective-permute-done | bytes 49184 | tf_op jit(solution)/shard_map/ppermute | solution.py:27
  40.9 0.1 multiply_reduce_fusion
  41.0 0.1 multiply_convert_fusion
  41.1 0.0 copy-start.2
  41.1 30.0 %all_to_all.20 = bf16[12,16,1536]{2,1,0:T(8,128)(2,1)S(1)} all-to-all(bf16[12,16,1536]{2,1,0:T(8,128)(2,1)S(1)} %broadcast_in_dim.2), channel_id=1, replica_groups=mesh['zl'=6,'y'=8,'c'=2,'zh'=2,'x'=4] {'zl','zh'}, dimensions={0} | all-to-all | bytes 1179648 | tf_op jit(solution)/shard_map/all_to_all | solution.py:32
  71.2 7.8 %collective-permute-start.1 = (bf16[192,1536]{1,0:T(8,128)(2,1)S(1)}, bf16[192,1536]{1,0:T(8,128)(2,1)S(1)}, u32[]{:S(2)}, u32[]{:S(2)}) collective-permute-start(bf16[192,1536]{1,0:T(8,128)(2,1)S(1)} %bitcast.20), channel_id=1, source_target_pairs={{0,8},{8,0},{1,9},{9,1},{2,10},{10,2},{3,11},{11,3},{4,12},{12,4},... | collective-permute-start | bytes 1769480 | tf_op jit(solution)/shard_map/ppermute | solution.py:27
  79.7 0.1 stack.23.place_ref
  79.8 0.8 collective-permute-done.1.other_ref
  80.6 0.0 all-gather.2.cloned.1.call-done.text_ref
  80.6 0.0 copy-start
  80.6 2.0 %copy-done = bf16[1024,1664]{1,0:T(8,128)(2,1)S(1)} copy-done((bf16[1024,1664]{1,0:T(8,128)(2,1)S(1)}, bf16[1024,1664]{1,0:T(8,128)(2,1)}, u32[]{:S(2)}) %copy-start) | copy-done | bytes 3407896
  82.5 0.0 copy-start.1
  82.5 2.9 %shard_map.88 = (f32[192,1024]{1,0:T(8,128)S(1)}, f32[32,1,1152]{2,1,0:T(1,128)S(1)}) custom-call(s32[5]{0:T(128)S(1)} %stack.23.place_ref, f32[1]{0:T(128)} %bitcast.5.scale_ref, bf16[192,1536]{1,0:T(8,128)(2,1)S(1)} %bitcast.21, bf16[192,1536]{1,0:T(8,128)(2,1)S(1)} %collective-permute-done.1.other_ref, bf16[1024,1664]{1,0:T(8,128)(2,1)S(1)} %copy-done), custom_call_target="tpu_custom_call" | custom-call | flops 1207959552 | bytes 3407872 | tf_op jit(solution)/shard_map/pallas_call | solution.py:170
  85.5 17.2 %all_to_all.21.stats_ref = f32[32,1,1152]{2,1,0:T(1,128)S(1)} all-to-all(f32[32,1,1152]{2,1,0:T(1,128)S(1)} %get-tuple-element.7), channel_id=1, replica_groups=mesh['zl'=6,'y'=8,'c'=2,'zh'=2,'x'=4] {'y','x'}, dimensions={0} | all-to-all | bytes 294912 | tf_op jit(solution)/shard_map/all_to_all | solution.py:245
  102.7 0.0 copy-done.2
  102.7 0.0 copy-done.1
  102.7 1.6 %shard_map.89 = (f32[1,128]{1,0:T(1,128)S(1)}, f32[96,1536]{1,0:T(8,128)S(1)}, bf16[96,1536]{1,0:T(8,128)(2,1)S(1)}) custom-call(s32[5]{0:T(128)S(1)} %stack.23.place_ref, s32[96]{0:T(128)S(1)} %copy-done.2, f32[32,1,1152]{2,1,0:T(1,128)S(1)} %all_to_all.21.stats_ref, f32[192,1024]{1,0:T(8,128)S(1)} %get-tuple-element.8.kept_ref, ...), custom_call_target="tpu_custom_call" | custom-call | flops 603979776 | bytes 3407872 | tf_op jit(solution)/shard_map/pallas_call | solution.py:170
  104.3 4.0 %collective-permute-start.2 = (bf16[96,1536]{1,0:T(8,128)(2,1)S(1)}, bf16[96,1536]{1,0:T(8,128)(2,1)S(1)}, u32[]{:S(2)}, u32[]{:S(2)}) collective-permute-start(bf16[96,1536]{1,0:T(8,128)(2,1)S(1)} %get-tuple-element.11), channel_id=1, source_target_pairs={{0,8},{8,0},{1,9},{9,1},{2,10},{10,2},{3,11},{11,3},{4,12},{12,4},... | collective-permute-start | bytes 884744 | tf_op jit(solution)/shard_map/ppermute | solution.py:27
  108.3 1.2 collective-permute-done.2
  109.5 0.8 add_convert_fusion
  110.3 3.5 %all-to-all-start.3 = ((bf16[6,16,1536]{2,1,0:T(8,128)(2,1)}), bf16[6,16,1536]{2,1,0:T(8,128)(2,1)S(1)}, u32[]{:S(2)}, u32[]{:S(2)}) async-start(bf16[6,16,1536]{2,1,0:T(8,128)(2,1)} %bitcast.12), calls=%async_computation.3 | async-start | bytes 589824 | tf_op jit(solution)/shard_map/all_to_all | solution.py:261
  113.7 0.6 dynamic-slice_bitcast_fusion
  114.3 13.4 %all-to-all-done.3 = bf16[6,16,1536]{2,1,0:T(8,128)(2,1)S(1)} async-done(((bf16[6,16,1536]{2,1,0:T(8,128)(2,1)}), bf16[6,16,1536]{2,1,0:T(8,128)(2,1)S(1)}, u32[]{:S(2)}, u32[]{:S(2)}) %all-to-all-start.3) | async-done | bytes 294944 | tf_op jit(solution)/shard_map/all_to_all | solution.py:261
  127.7 0.7 broadcast_multiply_fusion
  (4 shorter events, 0.1 us)
Async XLA Ops:
  7.2 73.4 %all-gather.2.cloned.1.call-start = ((), (), s32[]{:S(2)}) async-start(), calls=%async_computation.4 | async-start | bytes 3833856 | tf_op jit(solution)/shard_map/all_gather | solution.py:203
  12.7 11.1 %all-to-all-start = ((bf16[4,2,16,1536]{3,2,1,0:T(8,128)(2,1)}), bf16[4,2,16,1536]{3,2,1,0:T(8,128)(2,1)S(1)}, u32[]{:S(2)}, u32[]{:S(2)}) async-start(bf16[4,2,16,1536]{3,2,1,0:T(8,128)(2,1)} %shard_map.86), calls=%async_computation | async-start | bytes 786432 | tf_op jit(solution)/shard_map/all_to_all | solution.py:222
  23.9 17.0 %collective-permute-start = (bf16[16,1536]{1,0:T(8,128)(2,1)S(1)}, bf16[16,1536]{1,0:T(8,128)(2,1)S(1)}, u32[]{:S(2)}, u32[]{:S(2)}) collective-permute-start(bf16[16,1536]{1,0:T(8,128)(2,1)S(1)} %fusion), channel_id=1, source_target_pairs={{0,4},{4,0},{1,5},{5,1},{2,6},{6,2},{3,7},{7,3},{8,12},{12,8},{9,1... | collective-permute-start | bytes 147464 | tf_op jit(solution)/shard_map/ppermute | solution.py:27
  41.1 61.6 %copy-start.2 = (s32[96]{0:T(128)S(1)}, s32[96]{0:T(128)}, u32[]{:S(2)}) copy-start(s32[96]{0:T(128)} %count_ref.1) | copy-start | bytes 1156
  71.2 9.4 %collective-permute-start.1 = (bf16[192,1536]{1,0:T(8,128)(2,1)S(1)}, bf16[192,1536]{1,0:T(8,128)(2,1)S(1)}, u32[]{:S(2)}, u32[]{:S(2)}) collective-permute-start(bf16[192,1536]{1,0:T(8,128)(2,1)S(1)} %bitcast.20), channel_id=1, source_target_pairs={{0,8},{8,0},{1,9},{9,1},{2,10},{10,2},{3,11},{11,3},{4,12},{12,4},... | collective-permute-start | bytes 1769480 | tf_op jit(solution)/shard_map/ppermute | solution.py:27
  80.6 2.0 %copy-start = (bf16[1024,1664]{1,0:T(8,128)(2,1)S(1)}, bf16[1024,1664]{1,0:T(8,128)(2,1)}, u32[]{:S(2)}) copy-start(bf16[1024,1664]{1,0:T(8,128)(2,1)} %all-gather.2.cloned.1.call-done.text_ref) | copy-start | bytes 10223620
  82.5 20.1 %copy-start.1 = (bf16[1024,1664]{1,0:T(8,128)(2,1)S(1)}, bf16[1024,1664]{1,0:T(8,128)(2,1)}, u32[]{:S(2)}) copy-start(bf16[1024,1664]{1,0:T(8,128)(2,1)} %all-gather.2.cloned.1.call-done.text_ref) | copy-start | bytes 10223620
  104.3 5.2 %collective-permute-start.2 = (bf16[96,1536]{1,0:T(8,128)(2,1)S(1)}, bf16[96,1536]{1,0:T(8,128)(2,1)S(1)}, u32[]{:S(2)}, u32[]{:S(2)}) collective-permute-start(bf16[96,1536]{1,0:T(8,128)(2,1)S(1)} %get-tuple-element.11), channel_id=1, source_target_pairs={{0,8},{8,0},{1,9},{9,1},{2,10},{10,2},{3,11},{11,3},{4,12},{12,4},... | collective-permute-start | bytes 884744 | tf_op jit(solution)/shard_map/ppermute | solution.py:27
  110.3 17.4 %all-to-all-start.3 = ((bf16[6,16,1536]{2,1,0:T(8,128)(2,1)}), bf16[6,16,1536]{2,1,0:T(8,128)(2,1)S(1)}, u32[]{:S(2)}, u32[]{:S(2)}) async-start(bf16[6,16,1536]{2,1,0:T(8,128)(2,1)} %bitcast.12), calls=%async_computation.3 | async-start | bytes 589824 | tf_op jit(solution)/shard_map/all_to_all | solution.py:261
Sparse Core Ops, SparseCore 0:
  10.4 60.0 all-gather.1

commit v5 on v4

v5 whole, which is shorter than its diff:
```python
import functools

import jax
import jax.numpy as jnp
from jax import lax
from jax.experimental import pallas as pl
from jax.experimental.pallas import tpu as pltpu
from jax.sharding import Mesh, PartitionSpec as P

BATCH = ("zl", "y", "c")
TENSOR = ("zh", "x")
BF16 = jnp.bfloat16
F32 = jnp.float32
I32 = jnp.int32
VMEM = pl.BlockSpec(memory_space=pltpu.VMEM)
HBM = pl.BlockSpec(memory_space=pl.ANY)
SMEM = pl.BlockSpec(memory_space=pltpu.SMEM)
LAST = (((1,), (1,)), ((), ()))
INNER = (((1,), (0,)), ((), ()))


def unit_rows(values):
    return values * lax.rsqrt(jnp.sum(values * values, axis=1, keepdims=True) + 1e-06)


def swapped(value, axis):
    return lax.ppermute(value, axis, [(0, 1), (1, 0)])


def spread(value, axis, count):
    chunks = jnp.broadcast_to(value[None], (count,) + value.shape)
    return lax.all_to_all(chunks, axis, 0, 0)


def started(sems, *pairs):
    copies = [pltpu.make_async_copy(a, b, sems.at[i]) for i, (a, b) in enumerate(pairs)]
    for copy in copies:
        copy.start()
    return copies


def first_kernel(
    text_hbm, pair_hbm, audio_hbm, first_hbm, second_hbm, packed_ref, out_ref,
    text_ref, pair_ref, audio_ref, first_ref, second_ref, sems,
):
    rows, width = text_ref.shape
    n_x, n_zh, share, _ = out_ref.shape
    depth = audio_ref.shape[1]
    pieces = 4
    spans = [pl.ds(i * depth // pieces, depth // pieces) for i in range(pieces)]
    pairs = [(text_hbm, text_ref), (pair_hbm, pair_ref)]
    for span in spans:
        pairs.append((audio_hbm.at[:, span], audio_ref.at[:, span]))
        pairs.append((first_hbm.at[:, span], first_ref.at[:, span]))
    text_copy, pair_copy, *copies = started(sems, *pairs, (second_hbm, second_ref))
    pair_copy.wait()
    pair = pair_ref[...]
    half = rows // 2
    low = lax.rem(pair, rows).astype(F32)
    high = lax.div(pair, rows).astype(F32)
    packed_ref[:half, width:] = jnp.broadcast_to(low, (half, rows)).astype(BF16)
    packed_ref[half:, width:] = jnp.broadcast_to(high, (half, rows)).astype(BF16)
    text_copy.wait()
    packed_ref[:, :width] = unit_rows(text_ref[...].astype(F32)).astype(BF16)
    pre_act = 0.0
    for i, span in enumerate(spans):
        copies[2 * i].wait()
        copies[2 * i + 1].wait()
        pre_act += lax.dot_general(audio_ref[:, span], first_ref[:, span], LAST, preferred_element_type=F32)
    hidden = 0.5 * pre_act * (1.0 + lax.erf(pre_act * 0.7071067811865476))
    copies[-1].wait()
    partial = lax.dot_general(
        hidden.astype(BF16), second_ref[...], INNER, preferred_element_type=F32
    ).astype(BF16)
    for zh in range(n_zh):
        for x in range(n_x):
            start = (zh * n_x + x) * share
            out_ref[x, zh] = partial[start : start + share]


def pair_columns(text_ref, block, rows, width, place, sizes, share):
    zl, y, c, zh, x = place
    n_y, n_x = sizes
    start = block * rows
    low = text_ref[start : start + 16, width:].astype(F32)[0:1].astype(I32)
    start = start + rows // 2
    high = text_ref[start : start + 16, width:].astype(F32)[0:1].astype(I32)
    pair_t = lax.div(low, share)
    held = (lax.rem(lax.div(high, 2), n_y) == y) & (lax.rem(pair_t, n_x) == x)
    column = lax.div(high, 2 * n_y) * share + lax.rem(low, share)
    near_c = lax.rem(high, 2) == c
    return held, column, near_c, lax.div(pair_t, n_x)


def logits_kernel(scale_ref, audio_ref, text_ref, *refs, near, sizes, share):
    before, (kept_ref, stats_ref) = refs[:-2], refs[-2:]
    n_y, n_x = sizes
    audio_rows, width = audio_ref.shape
    rows = text_ref.shape[0] // n_y
    place = tuple(lax.axis_index(a) for a in BATCH + TENSOR)
    scale = scale_ref[0]
    n_zl = audio_rows // (2 * share)
    step = 2 * rows
    zh = place[3]
    row_ids = lax.broadcasted_iota(I32, (audio_rows, step), 0)
    for q in range(n_y // 2):
        span = slice(q * step, (q + 1) * step)
        columns = []
        for i in range(2):
            held, column, near_c, pair_zh = pair_columns(text_ref, 2 * q + i, rows, width, place, sizes, share)
            spot = lax.div(column, share) * 2 * share + lax.rem(column, share) + pair_zh * share
            columns.append(jnp.where(held & (near_c == near), spot, -1))
        column = jnp.concatenate(columns, axis=1)
        part = scale * lax.dot_general(
            audio_ref[...], text_ref[span, :width], LAST, preferred_element_type=F32
        )
        picked = jnp.sum(jnp.where(row_ids == column, part, 0.0), axis=0, keepdims=True)
        for zl in range(n_zl):
            both = part[2 * zl * share : 2 * (zl + 1) * share]
            kept_ref[zl * share : (zl + 1) * share, span] = jnp.where(zh == 0, both[:share], both[share:])
        top = jnp.max(part, axis=0, keepdims=True)
        if not before:
            stats_ref[0:1, span] = top
            stats_ref[1:2, span] = jnp.sum(jnp.exp(part - top), axis=0, keepdims=True)
            stats_ref[2:3, span] = picked
            continue
        top_before, mass, picked_before = (before[0][i : i + 1, span] for i in range(3))
        top = jnp.maximum(top, top_before)
        mass = mass * jnp.exp(top_before - top) + jnp.sum(jnp.exp(part - top), axis=0, keepdims=True)
        picked += picked_before
        local = top + jnp.log(mass)
        stats_ref[:, :, span] = jnp.broadcast_to(local[None], (n_y * n_x, 1, step))
        for i in range(2):
            first = (2 * q + i) * n_x
            block = picked[:, i * rows : (i + 1) * rows]
            stats_ref[first : first + n_x, :, n_y * rows :] = jnp.broadcast_to(block[None], (n_x, 1, rows))


def terms_kernel(count_ref, stats_ref, own_ref, other_ref, text_ref, loss_ref, near_ref, far_ref, weight_ref, *, sizes, share):
    n_y, n_x = sizes
    half, width = near_ref.shape
    rows = text_ref.shape[0] // n_y
    place = tuple(lax.axis_index(a) for a in BATCH + TENSOR)
    zl, y, c, zh, x = place
    stats = stats_ref[:, :, : n_y * rows]
    top = jnp.max(stats, axis=0)
    total = top + jnp.log(jnp.sum(jnp.exp(stats - top[None]), axis=0))
    picked = jnp.sum(stats_ref[:, :, n_y * rows :], axis=0)
    row_ids = lax.broadcasted_iota(I32, (half, rows), 0)
    lane_ids = lax.broadcasted_iota(I32, (1, rows), 1)
    loss = jnp.zeros((1, rows), F32)
    for block in range(n_y):
        span = slice(block * rows, (block + 1) * rows)
        valid = lane_ids < count_ref[(zl * n_y + block) * 2 + c]
        loss = jnp.where(valid & (y == block), total[:, span] - picked, loss)
        held, column, near_c, pair_zh = pair_columns(text_ref, block, rows, width, place, sizes, share)
        column = jnp.where(held & (pair_zh == zh), column, -1)
        for i, (ref, near) in enumerate(((own_ref, True), (other_ref, False))):
            hit = row_ids == jnp.where(near_c == near, column, -1)
            weights = jnp.exp(ref[:, span] - total[:, span]) - jnp.where(hit, 1.0, 0.0)
            weight_ref[i * half : (i + 1) * half, span] = jnp.where(valid, weights, 0.0).astype(BF16)
    loss_ref[...] = loss
    step = 512 if width % 512 == 0 else width
    for start in range(0, width, step):
        span = slice(start, start + step)
        terms = lax.dot_general(weight_ref[...], text_ref[:, span], INNER, preferred_element_type=F32)
        near_ref[:, span] = terms[:half]
        far_ref[:, span] = terms[half:].astype(BF16)


def call(kernel, outs, specs, *args, vmem=32, scratch=(), flops=0, moved=0):
    return pl.pallas_call(
        kernel,
        out_shape=outs,
        in_specs=specs,
        out_specs=jax.tree.map(lambda _: VMEM, outs),
        scratch_shapes=scratch,
        compiler_params=pltpu.CompilerParams(vmem_limit_bytes=vmem * 2**20),
        cost_estimate=pl.CostEstimate(flops=flops, bytes_accessed=moved, transcendentals=0),
    )(*args)


def on_device(audio_hidden, head_in, head_out, text_embed, log_scale, pair_index, valid_count):
    rows, width = text_embed.shape
    n_zl, n_y, n_zh, n_x = (lax.axis_size(a) for a in ("zl", "y", "zh", "x"))
    zh, x = lax.axis_index("zh"), lax.axis_index("x")
    share = rows // (n_zh * n_x)
    sizes = (n_y, n_x)
    scale = jnp.exp(log_scale)
    out = jax.ShapeDtypeStruct

    packed, partial = call(
        first_kernel,
        (out((rows, width + rows), BF16), out((n_x, n_zh, share, width), BF16)),
        [HBM] * 5,
        text_embed,
        pair_index.reshape(1, rows),
        audio_hidden,
        head_in.T,
        head_out,
        vmem=62,
        scratch=[
            pltpu.VMEM((rows, width), BF16),
            pltpu.VMEM((1, rows), I32),
            pltpu.VMEM(audio_hidden.shape, BF16),
            pltpu.VMEM(head_in.shape[::-1], BF16),
            pltpu.VMEM(head_out.shape, BF16),
            pltpu.SemaphoreType.DMA((11,)),
        ],
        flops=2 * rows * head_in.shape[1] * (head_in.shape[0] + width),
        moved=2 * (audio_hidden.size + head_in.size + head_out.size),
    )
    text = lax.all_gather(packed, "y", axis=0, tiled=True)

    partial = lax.all_to_all(partial, "x", 0, 0)
    halves = jnp.sum(partial.astype(F32), axis=0)
    mine = jnp.where(zh == 0, halves[0], halves[1])
    other = jnp.where(zh == 0, halves[1], halves[0])
    raw = mine + swapped(other.astype(BF16), "zh").astype(F32)
    audio_unit = unit_rows(raw).astype(BF16)

    own = spread(audio_unit, ("zl", "zh"), n_zl * n_zh).reshape(n_zl * n_zh * share, width)
    other = swapped(own, "c")
    half = n_zl * share

    def logits(near, audio, outs, *before):
        return call(
            functools.partial(logits_kernel, near=near, sizes=sizes, share=share),
            (out((half, n_y * rows), F32), outs),
            [SMEM] + [VMEM] * (2 + len(before)),
            scale.reshape(1),
            audio,
            text,
            *before,
            flops=4 * half * n_y * rows * width,
            moved=2 * text.size,
        )

    kept_own, sums = logits(True, own, out((8, n_y * rows), F32))
    kept_other, stats = logits(False, other, out((n_y * n_x, 1, (n_y + 1) * rows), F32), sums)
    stats = lax.all_to_all(stats, ("y", "x"), 0, 0)
    losses, near, far = call(
        functools.partial(terms_kernel, sizes=sizes, share=share),
        (out((1, rows), F32), out((half, width), F32), out((half, width), BF16)),
        [SMEM, VMEM, VMEM, VMEM, VMEM],
        valid_count,
        stats,
        kept_own,
        kept_other,
        text,
        scratch=[pltpu.VMEM((2 * half, n_y * rows), BF16)],
        flops=4 * half * n_y * rows * width,
        moved=2 * text.size,
    )
    row_loss = lax.dynamic_slice_in_dim(losses[0], (zh * n_x + x) * share, share, 0)
    near = near + swapped(far, "c").astype(F32)
    parts = lax.all_to_all(near.astype(BF16).reshape(n_zl, share, width), "zl", 0, 0)
    grad_audio = scale * jnp.sum(parts.astype(F32), axis=0)
    return (row_loss, grad_audio)


def build(mesh):
    placed = (
        P(BATCH, None),
        P(None, TENSOR),
        P(TENSOR, None),
        P(BATCH, None),
        P(),
        P(BATCH),
        P(),
    )
    return jax.shard_map(
        on_device,
        mesh=mesh,
        in_specs=placed,
        out_specs=(P(BATCH + TENSOR), P(BATCH + TENSOR, None)),
        check_vma=False,
    )


def solution(mesh):
    return build(Mesh(mesh.devices.reshape(6, 8, 2, 2, 4), BATCH + TENSOR))
```

time: 136 us -> 133 us (0.978)
  Pallas kernels: 9.99 us -> 7.91 us
    pallas_call x4, Pallas kernels: 9.99 us -> 7.91 us  [call(): pl.pallas_call(kernel, out_shape=outs, in_specs=specs, out_specs=jax.tree...]
  transfers between devices with their start and end apart: 6 -> 6, of which waited for: 5 -> 4; matrix products, arithmetic and copies ran while one was open for 1% -> 1% of each run, Pallas kernels for 3% -> 1%
where the time goes in v5:
time: 133 us
  blocking collectives  47.7 us (36%)
  starting transfers between devices  35.2 us (26%)
  waiting for transfers between devices  22.3 us (17%)
  between operations  14.8 us (11%)
  Pallas kernels  7.91 us (6%)
  local copies, waits for them, and re-layouts  3.24 us (2%)
  other arithmetic  1.75 us (1%)
    all_to_all x1, blocking collectives, spread(): return lax.all_to_all(chunks, axis, 0, 0)  30 us
    ppermute x3, starting transfers between devices, swapped(): return lax.ppermute(value, axis, [(0, 1), (1, 0)])  26.8 us
    all_to_all x1, blocking collectives, on_device(): stats = lax.all_to_all(stats, ('y', 'x'), 0, 0)  17.7 us
    all_to_all x1, waiting for transfers between devices, on_device(): lax.all_to_all(near.astype(BF16).reshape(n_zl, share, width), 'zl', 0, 0)  13.4 us
    pallas_call x4, Pallas kernels, call(): pl.pallas_call(kernel, out_shape=outs, in_specs=specs, out_specs=jax.tree...  7.91 us
    all_to_all x1, waiting for transfers between devices, on_device(): partial = lax.all_to_all(partial, 'x', 0, 0)  6.23 us
    all_to_all x1, starting transfers between devices, on_device(): partial = lax.all_to_all(partial, 'x', 0, 0)  4.87 us
    all_to_all x1, starting transfers between devices, on_device(): lax.all_to_all(near.astype(BF16).reshape(n_zl, share, width), 'zl', 0, 0)  3.47 us
  transfers between devices with their start and end apart: 6, of which 4 were waited for; matrix products, arithmetic and copies ran while one was open for 1% of the time, Pallas kernels for 1%

profile of v5, /device:TPU:1, one launch (start us, length us, event | category | flops | bytes accessed | tf_op | source)
XLA Modules:
  0.0 132.9 jit_solution(3451038682022966567)
XLA Ops:
  7.2 0.0 all-gather.2.cloned.1.call-start
  7.2 3.7 %shard_map.86 = (bf16[128,1664]{1,0:T(8,128)(2,1)}, bf16[4,2,16,1536]{3,2,1,0:T(8,128)(2,1)}) custom-call(bf16[128,1536]{1,0:T(8,128)(2,1)} %text_hbm.1, s32[1,128]{1,0:T(1,128)} %bitcast.18, bf16[128,4096]{1,0:T(8,128)(2,1)} %audio_hbm.1, bf16[192,4096]{1,0:T(8,128)(2,1)} %bitcast.17, bf16[192,1536]{1,0:T(8,128)(2,1)} %second_hbm.1), custom_call_target="tpu_custom_call" | custom-call | flops 276824064 | bytes 3211264 | tf_op jit(solution)/shard_map/pallas_call | solution.py:172
  10.9 0.0 all-gather.2.cloned.1.call-update
  10.9 4.9 %all-to-all-start = ((bf16[4,2,16,1536]{3,2,1,0:T(8,128)(2,1)}), bf16[4,2,16,1536]{3,2,1,0:T(8,128)(2,1)S(1)}, u32[]{:S(2)}, u32[]{:S(2)}) async-start(bf16[4,2,16,1536]{3,2,1,0:T(8,128)(2,1)} %get-tuple-element.11), calls=%async_computation | async-start | bytes 786432 | tf_op jit(solution)/shard_map/all_to_all | solution.py:215
  15.8 6.2 %all-to-all-done = bf16[4,2,16,1536]{3,2,1,0:T(8,128)(2,1)S(1)} async-done(((bf16[4,2,16,1536]{3,2,1,0:T(8,128)(2,1)}), bf16[4,2,16,1536]{3,2,1,0:T(8,128)(2,1)S(1)}, u32[]{:S(2)}, u32[]{:S(2)}) %all-to-all-start) | async-done | bytes 393248 | tf_op jit(solution)/shard_map/all_to_all | solution.py:215
  22.0 0.1 convert_reduce_fusion
  22.1 15.5 %collective-permute-start = (bf16[16,1536]{1,0:T(8,128)(2,1)S(1)}, bf16[16,1536]{1,0:T(8,128)(2,1)S(1)}, u32[]{:S(2)}, u32[]{:S(2)}) collective-permute-start(bf16[16,1536]{1,0:T(8,128)(2,1)S(1)} %fusion), channel_id=1, source_target_pairs={{0,4},{4,0},{1,5},{5,1},{2,6},{6,2},{3,7},{7,3},{8,12},{12,8},{9,1... | collective-permute-start | bytes 147464 | tf_op jit(solution)/shard_map/ppermute | solution.py:27
  37.6 1.5 %collective-permute-done = bf16[16,1536]{1,0:T(8,128)(2,1)S(1)} collective-permute-done((bf16[16,1536]{1,0:T(8,128)(2,1)S(1)}, bf16[16,1536]{1,0:T(8,128)(2,1)S(1)}, u32[]{:S(2)}, u32[]{:S(2)}) %collective-permute-start) | collective-permute-done | bytes 49184 | tf_op jit(solution)/shard_map/ppermute | solution.py:27
  39.1 0.1 multiply_reduce_fusion
  39.2 0.1 multiply_convert_fusion
  39.3 0.1 broadcast_in_dim.2
  39.4 30.0 %all_to_all.20 = bf16[12,16,1536]{2,1,0:T(8,128)(2,1)S(1)} all-to-all(bf16[12,16,1536]{2,1,0:T(8,128)(2,1)S(1)} %broadcast_in_dim.2), channel_id=1, replica_groups=mesh['zl'=6,'y'=8,'c'=2,'zh'=2,'x'=4] {'zl','zh'}, dimensions={0} | all-to-all | bytes 1179648 | tf_op jit(solution)/shard_map/all_to_all | solution.py:32
  69.4 7.8 %collective-permute-start.1 = (bf16[192,1536]{1,0:T(8,128)(2,1)S(1)}, bf16[192,1536]{1,0:T(8,128)(2,1)S(1)}, u32[]{:S(2)}, u32[]{:S(2)}) collective-permute-start(bf16[192,1536]{1,0:T(8,128)(2,1)S(1)} %bitcast.15), channel_id=1, source_target_pairs={{0,8},{8,0},{1,9},{9,1},{2,10},{10,2},{3,11},{11,3},{4,12},{12,4},... | collective-permute-start | bytes 1769480 | tf_op jit(solution)/shard_map/ppermute | solution.py:27
  77.9 0.0 all-gather.2.cloned.1.call-done.text_ref
  77.9 0.0 copy-start
  77.9 2.0 %copy-done = bf16[1024,1664]{1,0:T(8,128)(2,1)S(1)} copy-done((bf16[1024,1664]{1,0:T(8,128)(2,1)S(1)}, bf16[1024,1664]{1,0:T(8,128)(2,1)}, u32[]{:S(2)}) %copy-start) | copy-done | bytes 3407896
  79.9 0.0 copy-start.1
  79.9 0.0 copy-start.2
  79.9 1.3 shard_map.87
  81.2 0.0 collective-permute-done.1.audio_ref
  81.2 0.6 copy-done.1
  81.8 1.3 shard_map.88
  83.1 17.7 %all_to_all.21.stats_ref = f32[32,1,1152]{2,1,0:T(1,128)S(1)} all-to-all(f32[32,1,1152]{2,1,0:T(1,128)S(1)} %get-tuple-element.14), channel_id=1, replica_groups=mesh['zl'=6,'y'=8,'c'=2,'zh'=2,'x'=4] {'y','x'}, dimensions={0} | all-to-all | bytes 294912 | tf_op jit(solution)/shard_map/all_to_all | solution.py:241
  100.8 0.0 copy-done.2
  100.8 1.6 %shard_map.89 = (f32[1,128]{1,0:T(1,128)S(1)}, f32[96,1536]{1,0:T(8,128)S(1)}, bf16[96,1536]{1,0:T(8,128)(2,1)S(1)}) custom-call(s32[96]{0:T(128)S(1)} %copy-done.2, f32[32,1,1152]{2,1,0:T(1,128)S(1)} %all_to_all.21.stats_ref, f32[96,1024]{1,0:T(8,128)S(1)} %get-tuple-element.15.own_ref, f32[96,1024]{1,0:T(8,128)S(1)} %get-tuple-element.16.other_ref, ...), custom_call_target="tpu_custom_call" | custom-call | flops 603979776 | bytes 3407872 | tf_op jit(solution)/shard_map/pallas_call | solution.py:172
  102.5 3.5 %collective-permute-start.2 = (bf16[96,1536]{1,0:T(8,128)(2,1)S(1)}, bf16[96,1536]{1,0:T(8,128)(2,1)S(1)}, u32[]{:S(2)}, u32[]{:S(2)}) collective-permute-start(bf16[96,1536]{1,0:T(8,128)(2,1)S(1)} %get-tuple-element.19), channel_id=1, source_target_pairs={{0,8},{8,0},{1,9},{9,1},{2,10},{10,2},{3,11},{11,3},{4,12},{12,4},... | collective-permute-start | bytes 884744 | tf_op jit(solution)/shard_map/ppermute | solution.py:27
  106.0 1.2 collective-permute-done.2
  107.2 0.8 add_convert_fusion
  108.0 3.5 %all-to-all-start.3 = ((bf16[6,16,1536]{2,1,0:T(8,128)(2,1)}), bf16[6,16,1536]{2,1,0:T(8,128)(2,1)S(1)}, u32[]{:S(2)}, u32[]{:S(2)}) async-start(bf16[6,16,1536]{2,1,0:T(8,128)(2,1)} %bitcast.7), calls=%async_computation.3 | async-start | bytes 589824 | tf_op jit(solution)/shard_map/all_to_all | solution.py:257
  111.4 0.6 dynamic-slice_bitcast_fusion
  112.0 13.4 %all-to-all-done.3 = bf16[6,16,1536]{2,1,0:T(8,128)(2,1)S(1)} async-done(((bf16[6,16,1536]{2,1,0:T(8,128)(2,1)}), bf16[6,16,1536]{2,1,0:T(8,128)(2,1)S(1)}, u32[]{:S(2)}, u32[]{:S(2)}) %all-to-all-start.3) | async-done | bytes 294944 | tf_op jit(solution)/shard_map/all_to_all | solution.py:257
  125.4 0.7 broadcast_multiply_fusion
  (3 shorter events, 0.1 us)
Async XLA Ops:
  7.2 70.7 %all-gather.2.cloned.1.call-start = ((), (), s32[]{:S(2)}) async-start(), calls=%async_computation.4 | async-start | bytes 3833856 | tf_op jit(solution)/shard_map/all_gather | solution.py:213
  10.9 11.1 %all-to-all-start = ((bf16[4,2,16,1536]{3,2,1,0:T(8,128)(2,1)}), bf16[4,2,16,1536]{3,2,1,0:T(8,128)(2,1)S(1)}, u32[]{:S(2)}, u32[]{:S(2)}) async-start(bf16[4,2,16,1536]{3,2,1,0:T(8,128)(2,1)} %get-tuple-element.11), calls=%async_computation | async-start | bytes 786432 | tf_op jit(solution)/shard_map/all_to_all | solution.py:215
  22.1 17.0 %collective-permute-start = (bf16[16,1536]{1,0:T(8,128)(2,1)S(1)}, bf16[16,1536]{1,0:T(8,128)(2,1)S(1)}, u32[]{:S(2)}, u32[]{:S(2)}) collective-permute-start(bf16[16,1536]{1,0:T(8,128)(2,1)S(1)} %fusion), channel_id=1, source_target_pairs={{0,4},{4,0},{1,5},{5,1},{2,6},{6,2},{3,7},{7,3},{8,12},{12,8},{9,1... | collective-permute-start | bytes 147464 | tf_op jit(solution)/shard_map/ppermute | solution.py:27
  69.4 11.8 %collective-permute-start.1 = (bf16[192,1536]{1,0:T(8,128)(2,1)S(1)}, bf16[192,1536]{1,0:T(8,128)(2,1)S(1)}, u32[]{:S(2)}, u32[]{:S(2)}) collective-permute-start(bf16[192,1536]{1,0:T(8,128)(2,1)S(1)} %bitcast.15), channel_id=1, source_target_pairs={{0,8},{8,0},{1,9},{9,1},{2,10},{10,2},{3,11},{11,3},{4,12},{12,4},... | collective-permute-start | bytes 1769480 | tf_op jit(solution)/shard_map/ppermute | solution.py:27
  77.9 2.0 %copy-start = (bf16[1024,1664]{1,0:T(8,128)(2,1)S(1)}, bf16[1024,1664]{1,0:T(8,128)(2,1)}, u32[]{:S(2)}) copy-start(bf16[1024,1664]{1,0:T(8,128)(2,1)} %all-gather.2.cloned.1.call-done.text_ref) | copy-start | bytes 10223620
  79.9 2.0 %copy-start.1 = (bf16[1024,1664]{1,0:T(8,128)(2,1)S(1)}, bf16[1024,1664]{1,0:T(8,128)(2,1)}, u32[]{:S(2)}) copy-start(bf16[1024,1664]{1,0:T(8,128)(2,1)} %all-gather.2.cloned.1.call-done.text_ref) | copy-start | bytes 10223620
  79.9 21.0 %copy-start.2 = (s32[96]{0:T(128)S(1)}, s32[96]{0:T(128)}, u32[]{:S(2)}) copy-start(s32[96]{0:T(128)} %count_ref.1) | copy-start | bytes 1156
  102.5 4.7 %collective-permute-start.2 = (bf16[96,1536]{1,0:T(8,128)(2,1)S(1)}, bf16[96,1536]{1,0:T(8,128)(2,1)S(1)}, u32[]{:S(2)}, u32[]{:S(2)}) collective-permute-start(bf16[96,1536]{1,0:T(8,128)(2,1)S(1)} %get-tuple-element.19), channel_id=1, source_target_pairs={{0,8},{8,0},{1,9},{9,1},{2,10},{10,2},{3,11},{11,3},{4,12},{12,4},... | collective-permute-start | bytes 884744 | tf_op jit(solution)/shard_map/ppermute | solution.py:27
  108.0 17.4 %all-to-all-start.3 = ((bf16[6,16,1536]{2,1,0:T(8,128)(2,1)}), bf16[6,16,1536]{2,1,0:T(8,128)(2,1)S(1)}, u32[]{:S(2)}, u32[]{:S(2)}) async-start(bf16[6,16,1536]{2,1,0:T(8,128)(2,1)} %bitcast.7), calls=%async_computation.3 | async-start | bytes 589824 | tf_op jit(solution)/shard_map/all_to_all | solution.py:257
Sparse Core Ops, SparseCore 0:
  11.0 60.0 all-gather.1

commit v6 on v5

--- a/solution.py
+++ b/solution.py
@@ -98,7 +98,7 @@
     audio_rows, width = audio_ref.shape
     rows = text_ref.shape[0] // n_y
     place = tuple(lax.axis_index(a) for a in BATCH + TENSOR)
-    scale = scale_ref[0]
+    scale = scale_ref[...]
     n_zl = audio_rows // (2 * share)
     step = 2 * rows
     zh = place[3]
@@ -136,7 +136,7 @@
             stats_ref[first : first + n_x, :, n_y * rows :] = jnp.broadcast_to(block[None], (n_x, 1, rows))
 
 
-def terms_kernel(count_ref, stats_ref, own_ref, other_ref, text_ref, loss_ref, near_ref, far_ref, weight_ref, *, sizes, share):
+def terms_kernel(count_ref, scale_ref, stats_ref, own_ref, other_ref, text_ref, loss_ref, near_ref, far_ref, weight_ref, *, sizes, share):
     n_y, n_x = sizes
     half, width = near_ref.shape
     rows = text_ref.shape[0] // n_y
@@ -159,11 +159,14 @@
             hit = row_ids == jnp.where(near_c == near, column, -1)
             weights = jnp.exp(ref[:, span] - total[:, span]) - jnp.where(hit, 1.0, 0.0)
             weight_ref[i * half : (i + 1) * half, span] = jnp.where(valid, weights, 0.0).astype(BF16)
-    loss_ref[...] = loss
+    first = (zh * n_x + x) * share
+    loss_ref[...] = pltpu.roll(loss, lax.rem(rows - first, rows), 1)[:, :share]
     step = 512 if width % 512 == 0 else width
     for start in range(0, width, step):
         span = slice(start, start + step)
-        terms = lax.dot_general(weight_ref[...], text_ref[:, span], INNER, preferred_element_type=F32)
+        terms = scale_ref[...] * lax.dot_general(
+            weight_ref[...], text_ref[:, span], INNER, preferred_element_type=F32
+        )
         near_ref[:, span] = terms[:half]
         far_ref[:, span] = terms[half:].astype(BF16)
 
@@ -183,10 +186,10 @@
 def on_device(audio_hidden, head_in, head_out, text_embed, log_scale, pair_index, valid_count):
     rows, width = text_embed.shape
     n_zl, n_y, n_zh, n_x = (lax.axis_size(a) for a in ("zl", "y", "zh", "x"))
-    zh, x = lax.axis_index("zh"), lax.axis_index("x")
+    zh = lax.axis_index("zh")
     share = rows // (n_zh * n_x)
     sizes = (n_y, n_x)
-    scale = jnp.exp(log_scale)
+    scale = jnp.exp(log_scale).reshape(1, 1)
     out = jax.ShapeDtypeStruct
 
     packed, partial = call(
@@ -212,7 +215,7 @@
     )
     text = lax.all_gather(packed, "y", axis=0, tiled=True)
 
-    partial = lax.all_to_all(partial, "x", 0, 0)
+    partial, scale = lax.optimization_barrier((lax.all_to_all(partial, "x", 0, 0), scale))
     halves = jnp.sum(partial.astype(F32), axis=0)
     mine = jnp.where(zh == 0, halves[0], halves[1])
     other = jnp.where(zh == 0, halves[1], halves[0])
@@ -227,8 +230,8 @@
         return call(
             functools.partial(logits_kernel, near=near, sizes=sizes, share=share),
             (out((half, n_y * rows), F32), outs),
-            [SMEM] + [VMEM] * (2 + len(before)),
-            scale.reshape(1),
+            [VMEM] * (3 + len(before)),
+            scale,
             audio,
             text,
             *before,
@@ -241,9 +244,10 @@
     stats = lax.all_to_all(stats, ("y", "x"), 0, 0)
     losses, near, far = call(
         functools.partial(terms_kernel, sizes=sizes, share=share),
-        (out((1, rows), F32), out((half, width), F32), out((half, width), BF16)),
-        [SMEM, VMEM, VMEM, VMEM, VMEM],
+        (out((1, share), F32), out((half, width), F32), out((half, width), BF16)),
+        [SMEM] + [VMEM] * 5,
         valid_count,
+        scale,
         stats,
         kept_own,
         kept_other,
@@ -252,11 +256,10 @@
         flops=4 * half * n_y * rows * width,
         moved=2 * text.size,
     )
-    row_loss = lax.dynamic_slice_in_dim(losses[0], (zh * n_x + x) * share, share, 0)
     near = near + swapped(far, "c").astype(F32)
     parts = lax.all_to_all(near.astype(BF16).reshape(n_zl, share, width), "zl", 0, 0)
-    grad_audio = scale * jnp.sum(parts.astype(F32), axis=0)
-    return (row_loss, grad_audio)
+    grad_audio = jnp.sum(parts.astype(F32), axis=0)
+    return (losses[0], grad_audio)
 
 
 def build(mesh):

time: 133 us -> 133 us (level)
  blocking collectives: 47.7 us -> 65.2 us
  waiting for transfers between devices: 22.3 us -> 8.28 us
  starting transfers between devices: 35.2 us -> 31.8 us
    all_to_all x0 -> x1, blocking collectives: none -> 17.5 us  [on_device(): lax.all_to_all(near.astype(BF16).reshape(n_zl, share, width), 'zl', 0, 0)]
    all_to_all x2 -> x1, waiting for transfers between devices: 19.6 us -> 5.54 us  [on_device(): lax.all_to_all(partial, 'x', 0, 0)]
    all_to_all x2 -> x1, starting transfers between devices: 8.34 us -> 4.87 us  [on_device(): lax.all_to_all(partial, 'x', 0, 0)]
  transfers between devices with their start and end apart: 6 -> 5, of which waited for: 4 -> 3; matrix products, arithmetic and copies ran while one was open for 1% -> 0% of each run, Pallas kernels for 1% -> 1%
where the time goes in v6:
time: 133 us; the launch traced here: 132 us
  blocking collectives  65.2 us (49%)
  starting transfers between devices  31.8 us (24%)
  between operations  14.8 us (11%)
  waiting for transfers between devices  8.28 us (6%)
  Pallas kernels  8.26 us (6%)
  local copies, waits for them, and re-layouts  2.66 us (2%)
    all_to_all x1, blocking collectives, spread(): return lax.all_to_all(chunks, axis, 0, 0)  30 us
    ppermute x3, starting transfers between devices, swapped(): return lax.ppermute(value, axis, [(0, 1), (1, 0)])  26.9 us
    all_to_all x1, blocking collectives, on_device(): stats = lax.all_to_all(stats, ('y', 'x'), 0, 0)  17.7 us
    all_to_all x1, blocking collectives, on_device(): lax.all_to_all(near.astype(BF16).reshape(n_zl, share, width), 'zl', 0, 0)  17.5 us
    pallas_call x4, Pallas kernels, call(): pl.pallas_call(kernel, out_shape=outs, in_specs=specs, out_specs=jax.tree...  8.26 us
    all_to_all x1, waiting for transfers between devices, on_device(): lax.all_to_all(partial, 'x', 0, 0)  5.54 us
    all_to_all x1, starting transfers between devices, on_device(): lax.all_to_all(partial, 'x', 0, 0)  4.87 us
    ppermute x3, waiting for transfers between devices, swapped(): return lax.ppermute(value, axis, [(0, 1), (1, 0)])  2.7 us
  transfers between devices with their start and end apart: 5, of which 3 were waited for; matrix products, arithmetic and copies ran while one was open for 0% of the time, Pallas kernels for 1%

profile of v6, /device:TPU:1, one launch (start us, length us, event | category | flops | bytes accessed | tf_op | source)
XLA Modules:
  0.0 132.1 jit_solution(7054856464431088424)
XLA Ops:
  7.2 0.0 all-gather.2.cloned.1.call-start
  7.2 3.7 %shard_map.86 = (bf16[128,1664]{1,0:T(8,128)(2,1)}, bf16[4,2,16,1536]{3,2,1,0:T(8,128)(2,1)}) custom-call(bf16[128,1536]{1,0:T(8,128)(2,1)} %text_hbm.1, s32[1,128]{1,0:T(1,128)} %bitcast.18, bf16[128,4096]{1,0:T(8,128)(2,1)} %audio_hbm.1, bf16[192,4096]{1,0:T(8,128)(2,1)} %bitcast.16, bf16[192,1536]{1,0:T(8,128)(2,1)} %second_hbm.1), custom_call_target="tpu_custom_call" | custom-call | flops 276824064 | bytes 3211264 | tf_op jit(solution)/shard_map/pallas_call | solution.py:175
  10.9 0.0 all-gather.2.cloned.1.call-update
  10.9 4.9 %all-to-all-start = ((bf16[4,2,16,1536]{3,2,1,0:T(8,128)(2,1)}), bf16[4,2,16,1536]{3,2,1,0:T(8,128)(2,1)S(1)}, u32[]{:S(2)}, u32[]{:S(2)}) async-start(bf16[4,2,16,1536]{3,2,1,0:T(8,128)(2,1)} %get-tuple-element.13), calls=%async_computation | async-start | bytes 786432 | tf_op jit(solution)/shard_map/all_to_all | solution.py:218
  16.5 5.5 %all-to-all-done = bf16[4,2,16,1536]{3,2,1,0:T(8,128)(2,1)S(1)} async-done(((bf16[4,2,16,1536]{3,2,1,0:T(8,128)(2,1)}), bf16[4,2,16,1536]{3,2,1,0:T(8,128)(2,1)S(1)}, u32[]{:S(2)}, u32[]{:S(2)}) %all-to-all-start) | async-done | bytes 393248 | tf_op jit(solution)/shard_map/all_to_all | solution.py:218
  22.0 0.1 convert_reduce_fusion
  22.1 15.5 %collective-permute-start = (bf16[16,1536]{1,0:T(8,128)(2,1)S(1)}, bf16[16,1536]{1,0:T(8,128)(2,1)S(1)}, u32[]{:S(2)}, u32[]{:S(2)}) collective-permute-start(bf16[16,1536]{1,0:T(8,128)(2,1)S(1)} %fusion), channel_id=1, source_target_pairs={{0,4},{4,0},{1,5},{5,1},{2,6},{6,2},{3,7},{7,3},{8,12},{12,8},{9,1... | collective-permute-start | bytes 147464 | tf_op jit(solution)/shard_map/ppermute | solution.py:27
  37.6 1.5 %collective-permute-done = bf16[16,1536]{1,0:T(8,128)(2,1)S(1)} collective-permute-done((bf16[16,1536]{1,0:T(8,128)(2,1)S(1)}, bf16[16,1536]{1,0:T(8,128)(2,1)S(1)}, u32[]{:S(2)}, u32[]{:S(2)}) %collective-permute-start) | collective-permute-done | bytes 49184 | tf_op jit(solution)/shard_map/ppermute | solution.py:27
  39.1 0.1 multiply_reduce_fusion
  39.2 0.1 multiply_convert_fusion
  39.3 0.1 broadcast_in_dim.2
  39.4 30.0 %all_to_all.20 = bf16[12,16,1536]{2,1,0:T(8,128)(2,1)S(1)} all-to-all(bf16[12,16,1536]{2,1,0:T(8,128)(2,1)S(1)} %broadcast_in_dim.2), channel_id=1, replica_groups=mesh['zl'=6,'y'=8,'c'=2,'zh'=2,'x'=4] {'zl','zh'}, dimensions={0} | all-to-all | bytes 1179648 | tf_op jit(solution)/shard_map/all_to_all | solution.py:32
  69.4 0.0 copy-start.2
  69.4 7.9 %collective-permute-start.1 = (bf16[192,1536]{1,0:T(8,128)(2,1)S(1)}, bf16[192,1536]{1,0:T(8,128)(2,1)S(1)}, u32[]{:S(2)}, u32[]{:S(2)}) collective-permute-start(bf16[192,1536]{1,0:T(8,128)(2,1)S(1)} %bitcast.14), channel_id=1, source_target_pairs={{0,8},{8,0},{1,9},{9,1},{2,10},{10,2},{3,11},{11,3},{4,12},{12,4},... | collective-permute-start | bytes 1769480 | tf_op jit(solution)/shard_map/ppermute | solution.py:27
  77.3 0.0 all-gather.2.cloned.1.call-done.text_ref
  77.3 0.0 copy-start
  77.3 2.0 %copy-done = bf16[1024,1664]{1,0:T(8,128)(2,1)S(1)} copy-done((bf16[1024,1664]{1,0:T(8,128)(2,1)S(1)}, bf16[1024,1664]{1,0:T(8,128)(2,1)}, u32[]{:S(2)}) %copy-start) | copy-done | bytes 3407896
  79.3 0.0 copy-start.1
  79.3 1.3 shard_map.87
  80.6 0.0 collective-permute-done.1.audio_ref
  80.6 0.7 copy-done.1
  81.3 1.3 %shard_map.88 = (f32[96,1024]{1,0:T(8,128)S(1)}, f32[32,1,1152]{2,1,0:T(1,128)S(1)}) custom-call(f32[1,1]{1,0:T(1,128)} %bitcast.2.scale_ref, bf16[192,1536]{1,0:T(8,128)(2,1)S(1)} %collective-permute-done.1.audio_ref, bf16[1024,1664]{1,0:T(8,128)(2,1)S(1)} %copy-done.1, f32[8,1024]{1,0:T(8,128)S(1)} %get-tuple-element.17.refs_0_), custom_call_target="tpu_custom_call" | custom-call | flops 603979776 | bytes 3407872 | tf_op jit(solution)/shard_map/pallas_call | solution.py:175
  82.6 17.7 %all_to_all.21.stats_ref = f32[32,1,1152]{2,1,0:T(1,128)S(1)} all-to-all(f32[32,1,1152]{2,1,0:T(1,128)S(1)} %get-tuple-element.18), channel_id=1, replica_groups=mesh['zl'=6,'y'=8,'c'=2,'zh'=2,'x'=4] {'y','x'}, dimensions={0} | all-to-all | bytes 294912 | tf_op jit(solution)/shard_map/all_to_all | solution.py:244
  100.3 0.0 copy-done.2
  100.3 2.0 %shard_map.89 = (f32[1,16]{1,0:T(1,128)}, f32[96,1536]{1,0:T(8,128)S(1)}, bf16[96,1536]{1,0:T(8,128)(2,1)S(1)}) custom-call(s32[96]{0:T(128)S(1)} %copy-done.2, f32[1,1]{1,0:T(1,128)} %bitcast.2.scale_ref, f32[32,1,1152]{2,1,0:T(1,128)S(1)} %all_to_all.21.stats_ref, f32[96,1024]{1,0:T(8,128)S(1)} %get-tuple-element.19.own_ref, ...), custom_call_target="tpu_custom_call" | custom-call | flops 603979776 | bytes 3407872 | tf_op jit(solution)/shard_map/pallas_call | solution.py:175
  102.3 3.5 %collective-permute-start.2 = (bf16[96,1536]{1,0:T(8,128)(2,1)S(1)}, bf16[96,1536]{1,0:T(8,128)(2,1)S(1)}, u32[]{:S(2)}, u32[]{:S(2)}) collective-permute-start(bf16[96,1536]{1,0:T(8,128)(2,1)S(1)} %get-tuple-element.23), channel_id=1, source_target_pairs={{0,8},{8,0},{1,9},{9,1},{2,10},{10,2},{3,11},{11,3},{4,12},{12,4},... | collective-permute-start | bytes 884744 | tf_op jit(solution)/shard_map/ppermute | solution.py:27
  105.8 1.2 collective-permute-done.2
  107.0 0.1 add_convert_fusion
  107.0 17.5 %all_to_all.22 = bf16[6,16,1536]{2,1,0:T(8,128)(2,1)S(1)} all-to-all(bf16[6,16,1536]{2,1,0:T(8,128)(2,1)S(1)} %bitcast.17), channel_id=1, replica_groups=mesh['zl'=6,'y'=8,'c'=2,'zh'=2,'x'=4] {'zl'}, dimensions={0} | all-to-all | bytes 589824 | tf_op jit(solution)/shard_map/all_to_all | solution.py:260
  124.5 0.7 convert_reduce_fusion.1
  (2 shorter events, 0.0 us)
Async XLA Ops:
  7.2 70.2 %all-gather.2.cloned.1.call-start = ((), (), s32[]{:S(2)}) async-start(), calls=%async_computation.4 | async-start | bytes 3833856 | tf_op jit(solution)/shard_map/all_gather | solution.py:216
  10.9 11.1 %all-to-all-start = ((bf16[4,2,16,1536]{3,2,1,0:T(8,128)(2,1)}), bf16[4,2,16,1536]{3,2,1,0:T(8,128)(2,1)S(1)}, u32[]{:S(2)}, u32[]{:S(2)}) async-start(bf16[4,2,16,1536]{3,2,1,0:T(8,128)(2,1)} %get-tuple-element.13), calls=%async_computation | async-start | bytes 786432 | tf_op jit(solution)/shard_map/all_to_all | solution.py:218
  22.1 17.0 %collective-permute-start = (bf16[16,1536]{1,0:T(8,128)(2,1)S(1)}, bf16[16,1536]{1,0:T(8,128)(2,1)S(1)}, u32[]{:S(2)}, u32[]{:S(2)}) collective-permute-start(bf16[16,1536]{1,0:T(8,128)(2,1)S(1)} %fusion), channel_id=1, source_target_pairs={{0,4},{4,0},{1,5},{5,1},{2,6},{6,2},{3,7},{7,3},{8,12},{12,8},{9,1... | collective-permute-start | bytes 147464 | tf_op jit(solution)/shard_map/ppermute | solution.py:27
  69.4 31.0 %copy-start.2 = (s32[96]{0:T(128)S(1)}, s32[96]{0:T(128)}, u32[]{:S(2)}) copy-start(s32[96]{0:T(128)} %count_ref.1) | copy-start | bytes 1156
  69.4 11.2 %collective-permute-start.1 = (bf16[192,1536]{1,0:T(8,128)(2,1)S(1)}, bf16[192,1536]{1,0:T(8,128)(2,1)S(1)}, u32[]{:S(2)}, u32[]{:S(2)}) collective-permute-start(bf16[192,1536]{1,0:T(8,128)(2,1)S(1)} %bitcast.14), channel_id=1, source_target_pairs={{0,8},{8,0},{1,9},{9,1},{2,10},{10,2},{3,11},{11,3},{4,12},{12,4},... | collective-permute-start | bytes 1769480 | tf_op jit(solution)/shard_map/ppermute | solution.py:27
  77.3 2.0 %copy-start = (bf16[1024,1664]{1,0:T(8,128)(2,1)S(1)}, bf16[1024,1664]{1,0:T(8,128)(2,1)}, u32[]{:S(2)}) copy-start(bf16[1024,1664]{1,0:T(8,128)(2,1)} %all-gather.2.cloned.1.call-done.text_ref) | copy-start | bytes 10223620
  79.3 2.0 %copy-start.1 = (bf16[1024,1664]{1,0:T(8,128)(2,1)S(1)}, bf16[1024,1664]{1,0:T(8,128)(2,1)}, u32[]{:S(2)}) copy-start(bf16[1024,1664]{1,0:T(8,128)(2,1)} %all-gather.2.cloned.1.call-done.text_ref) | copy-start | bytes 10223620
  102.3 4.7 %collective-permute-start.2 = (bf16[96,1536]{1,0:T(8,128)(2,1)S(1)}, bf16[96,1536]{1,0:T(8,128)(2,1)S(1)}, u32[]{:S(2)}, u32[]{:S(2)}) collective-permute-start(bf16[96,1536]{1,0:T(8,128)(2,1)S(1)} %get-tuple-element.23), channel_id=1, source_target_pairs={{0,8},{8,0},{1,9},{9,1},{2,10},{10,2},{3,11},{11,3},{4,12},{12,4},... | collective-permute-start | bytes 884744 | tf_op jit(solution)/shard_map/ppermute | solution.py:27
Sparse Core Ops, SparseCore 0:
  11.0 60.0 all-gather.1

commit v7 on v6

--- a/solution.py
+++ b/solution.py
@@ -136,39 +136,44 @@
             stats_ref[first : first + n_x, :, n_y * rows :] = jnp.broadcast_to(block[None], (n_x, 1, rows))
 
 
-def terms_kernel(count_ref, scale_ref, stats_ref, own_ref, other_ref, text_ref, loss_ref, near_ref, far_ref, weight_ref, *, sizes, share):
+def terms_kernel(count_ref, scale_ref, stats_ref, kept_ref, text_ref, *refs, near, sizes, share):
+    if near:
+        total_ref, loss_ref, terms_ref, weight_ref = refs
+    else:
+        total_ref, terms_ref, weight_ref = refs
     n_y, n_x = sizes
-    half, width = near_ref.shape
+    half, width = terms_ref.shape
     rows = text_ref.shape[0] // n_y
-    place = tuple(lax.axis_index(a) for a in BATCH + TENSOR)
-    zl, y, c, zh, x = place
-    stats = stats_ref[:, :, : n_y * rows]
-    top = jnp.max(stats, axis=0)
-    total = top + jnp.log(jnp.sum(jnp.exp(stats - top[None]), axis=0))
-    picked = jnp.sum(stats_ref[:, :, n_y * rows :], axis=0)
+    zl, y, c, zh, x = place = tuple(lax.axis_index(a) for a in BATCH + TENSOR)
+    if not near:
+        stats = stats_ref[:, :, : n_y * rows]
+        top = jnp.max(stats, axis=0)
+        total_ref[...] = top + jnp.log(jnp.sum(jnp.exp(stats - top[None]), axis=0))
+    total = total_ref[...]
     row_ids = lax.broadcasted_iota(I32, (half, rows), 0)
     lane_ids = lax.broadcasted_iota(I32, (1, rows), 1)
-    loss = jnp.zeros((1, rows), F32)
+    if near:
+        picked = jnp.sum(stats_ref[:, :, n_y * rows :], axis=0)
+        loss = jnp.zeros((1, rows), F32)
     for block in range(n_y):
         span = slice(block * rows, (block + 1) * rows)
         valid = lane_ids < count_ref[(zl * n_y + block) * 2 + c]
-        loss = jnp.where(valid & (y == block), total[:, span] - picked, loss)
+        if near:
+            loss = jnp.where(valid & (y == block), total[:, span] - picked, loss)
         held, column, near_c, pair_zh = pair_columns(text_ref, block, rows, width, place, sizes, share)
-        column = jnp.where(held & (pair_zh == zh), column, -1)
-        for i, (ref, near) in enumerate(((own_ref, True), (other_ref, False))):
-            hit = row_ids == jnp.where(near_c == near, column, -1)
-            weights = jnp.exp(ref[:, span] - total[:, span]) - jnp.where(hit, 1.0, 0.0)
-            weight_ref[i * half : (i + 1) * half, span] = jnp.where(valid, weights, 0.0).astype(BF16)
-    first = (zh * n_x + x) * share
-    loss_ref[...] = pltpu.roll(loss, lax.rem(rows - first, rows), 1)[:, :share]
+        hit = row_ids == jnp.where(held & (pair_zh == zh) & (near_c == near), column, -1)
+        weights = jnp.exp(kept_ref[:, span] - total[:, span]) - jnp.where(hit, 1.0, 0.0)
+        weight_ref[:, span] = jnp.where(valid, weights, 0.0).astype(BF16)
+    if near:
+        first = (zh * n_x + x) * share
+        loss_ref[...] = pltpu.roll(loss, lax.rem(rows - first, rows), 1)[:, :share]
     step = 512 if width % 512 == 0 else width
     for start in range(0, width, step):
         span = slice(start, start + step)
         terms = scale_ref[...] * lax.dot_general(
             weight_ref[...], text_ref[:, span], INNER, preferred_element_type=F32
         )
-        near_ref[:, span] = terms[:half]
-        far_ref[:, span] = terms[half:].astype(BF16)
+        terms_ref[:, span] = terms.astype(terms_ref.dtype)
 
 
 def call(kernel, outs, specs, *args, vmem=32, scratch=(), flops=0, moved=0):
@@ -242,21 +247,26 @@
     kept_own, sums = logits(True, own, out((8, n_y * rows), F32))
     kept_other, stats = logits(False, other, out((n_y * n_x, 1, (n_y + 1) * rows), F32), sums)
     stats = lax.all_to_all(stats, ("y", "x"), 0, 0)
-    losses, near, far = call(
-        functools.partial(terms_kernel, sizes=sizes, share=share),
-        (out((1, share), F32), out((half, width), F32), out((half, width), BF16)),
-        [SMEM] + [VMEM] * 5,
-        valid_count,
-        scale,
-        stats,
-        kept_own,
-        kept_other,
-        text,
-        scratch=[pltpu.VMEM((2 * half, n_y * rows), BF16)],
-        flops=4 * half * n_y * rows * width,
-        moved=2 * text.size,
-    )
-    near = near + swapped(far, "c").astype(F32)
+    def terms(near, kept, outs, *before):
+        return call(
+            functools.partial(terms_kernel, near=near, sizes=sizes, share=share),
+            outs,
+            [SMEM] + [VMEM] * (4 + len(before)),
+            valid_count,
+            scale,
+            stats,
+            kept,
+            text,
+            *before,
+            scratch=[pltpu.VMEM((half, n_y * rows), BF16)],
+            flops=2 * half * n_y * rows * width,
+            moved=2 * text.size,
+        )
+
+    total, far = terms(False, kept_other, (out((1, n_y * rows), F32), out((half, width), BF16)))
+    far = swapped(far, "c")
+    losses, near = terms(True, kept_own, (out((1, share), F32), out((half, width), F32)), total)
+    near = near + far.astype(F32)
     parts = lax.all_to_all(near.astype(BF16).reshape(n_zl, share, width), "zl", 0, 0)
     grad_audio = jnp.sum(parts.astype(F32), axis=0)
     return (losses[0], grad_audio)

time: 133 us -> 133 us (level)
    pallas_call x4 -> x5, Pallas kernels: 8.26 us -> 9.33 us  [call(): pl.pallas_call(kernel, out_shape=outs, in_specs=specs, out_specs=jax.tree...]
  transfers between devices with their start and end apart: 5 -> 5, of which waited for: 3 -> 2; matrix products, arithmetic and copies ran while one was open for 0% -> 0% of each run, Pallas kernels for 1% -> 2%
where the time goes in v7:
time: 133 us; the launch traced here: 132 us
  blocking collectives  65.5 us (49%)
  starting transfers between devices  31.8 us (24%)
  between operations  14.8 us (11%)
  Pallas kernels  9.33 us (7%)
  waiting for transfers between devices  7.09 us (5%)
  local copies, waits for them, and re-layouts  2.66 us (2%)
    all_to_all x1, blocking collectives, spread(): return lax.all_to_all(chunks, axis, 0, 0)  30 us
    ppermute x3, starting transfers between devices, swapped(): return lax.ppermute(value, axis, [(0, 1), (1, 0)])  26.9 us
    all_to_all x1, blocking collectives, on_device(): lax.all_to_all(near.astype(BF16).reshape(n_zl, share, width), 'zl', 0, 0)  17.8 us
    all_to_all x1, blocking collectives, on_device(): stats = lax.all_to_all(stats, ('y', 'x'), 0, 0)  17.7 us
    pallas_call x5, Pallas kernels, call(): pl.pallas_call(kernel, out_shape=outs, in_specs=specs, out_specs=jax.tree...  9.33 us
    all_to_all x1, waiting for transfers between devices, on_device(): lax.all_to_all(partial, 'x', 0, 0)  5.54 us
    all_to_all x1, starting transfers between devices, on_device(): lax.all_to_all(partial, 'x', 0, 0)  4.87 us
  transfers between devices with their start and end apart: 5, of which 2 were waited for; matrix products, arithmetic and copies ran while one was open for 0% of the time, Pallas kernels for 2%

profile of v7, /device:TPU:1, one launch (start us, length us, event | category | flops | bytes accessed | tf_op | source)
XLA Modules:
  0.0 132.3 jit_solution(10789645924724073304)
XLA Ops:
  7.2 0.0 all-gather.2.cloned.1.call-start
  7.2 3.7 %shard_map.86 = (bf16[128,1664]{1,0:T(8,128)(2,1)}, bf16[4,2,16,1536]{3,2,1,0:T(8,128)(2,1)}) custom-call(bf16[128,1536]{1,0:T(8,128)(2,1)} %text_hbm.1, s32[1,128]{1,0:T(1,128)} %bitcast.18, bf16[128,4096]{1,0:T(8,128)(2,1)} %audio_hbm.1, bf16[192,4096]{1,0:T(8,128)(2,1)} %bitcast.16, bf16[192,1536]{1,0:T(8,128)(2,1)} %second_hbm.1), custom_call_target="tpu_custom_call" | custom-call | flops 276824064 | bytes 3211264 | tf_op jit(solution)/shard_map/pallas_call | solution.py:180
  10.9 0.0 all-gather.2.cloned.1.call-update
  10.9 4.9 %all-to-all-start = ((bf16[4,2,16,1536]{3,2,1,0:T(8,128)(2,1)}), bf16[4,2,16,1536]{3,2,1,0:T(8,128)(2,1)S(1)}, u32[]{:S(2)}, u32[]{:S(2)}) async-start(bf16[4,2,16,1536]{3,2,1,0:T(8,128)(2,1)} %get-tuple-element.14), calls=%async_computation | async-start | bytes 786432 | tf_op jit(solution)/shard_map/all_to_all | solution.py:223
  16.5 5.5 %all-to-all-done = bf16[4,2,16,1536]{3,2,1,0:T(8,128)(2,1)S(1)} async-done(((bf16[4,2,16,1536]{3,2,1,0:T(8,128)(2,1)}), bf16[4,2,16,1536]{3,2,1,0:T(8,128)(2,1)S(1)}, u32[]{:S(2)}, u32[]{:S(2)}) %all-to-all-start) | async-done | bytes 393248 | tf_op jit(solution)/shard_map/all_to_all | solution.py:223
  22.0 0.1 convert_reduce_fusion
  22.1 15.5 %collective-permute-start = (bf16[16,1536]{1,0:T(8,128)(2,1)S(1)}, bf16[16,1536]{1,0:T(8,128)(2,1)S(1)}, u32[]{:S(2)}, u32[]{:S(2)}) collective-permute-start(bf16[16,1536]{1,0:T(8,128)(2,1)S(1)} %fusion), channel_id=1, source_target_pairs={{0,4},{4,0},{1,5},{5,1},{2,6},{6,2},{3,7},{7,3},{8,12},{12,8},{9,1... | collective-permute-start | bytes 147464 | tf_op jit(solution)/shard_map/ppermute | solution.py:27
  37.6 1.5 %collective-permute-done = bf16[16,1536]{1,0:T(8,128)(2,1)S(1)} collective-permute-done((bf16[16,1536]{1,0:T(8,128)(2,1)S(1)}, bf16[16,1536]{1,0:T(8,128)(2,1)S(1)}, u32[]{:S(2)}, u32[]{:S(2)}) %collective-permute-start) | collective-permute-done | bytes 49184 | tf_op jit(solution)/shard_map/ppermute | solution.py:27
  39.1 0.1 multiply_reduce_fusion
  39.2 0.1 multiply_convert_fusion
  39.3 0.1 broadcast_in_dim.2
  39.4 30.0 %all_to_all.20 = bf16[12,16,1536]{2,1,0:T(8,128)(2,1)S(1)} all-to-all(bf16[12,16,1536]{2,1,0:T(8,128)(2,1)S(1)} %broadcast_in_dim.2), channel_id=1, replica_groups=mesh['zl'=6,'y'=8,'c'=2,'zh'=2,'x'=4] {'zl','zh'}, dimensions={0} | all-to-all | bytes 1179648 | tf_op jit(solution)/shard_map/all_to_all | solution.py:32
  69.4 0.0 copy-start.2
  69.4 7.9 %collective-permute-start.1 = (bf16[192,1536]{1,0:T(8,128)(2,1)S(1)}, bf16[192,1536]{1,0:T(8,128)(2,1)S(1)}, u32[]{:S(2)}, u32[]{:S(2)}) collective-permute-start(bf16[192,1536]{1,0:T(8,128)(2,1)S(1)} %bitcast.14), channel_id=1, source_target_pairs={{0,8},{8,0},{1,9},{9,1},{2,10},{10,2},{3,11},{11,3},{4,12},{12,4},... | collective-permute-start | bytes 1769480 | tf_op jit(solution)/shard_map/ppermute | solution.py:27
  77.3 0.0 all-gather.2.cloned.1.call-done.text_ref
  77.3 0.0 copy-start
  77.4 2.0 %copy-done = bf16[1024,1664]{1,0:T(8,128)(2,1)S(1)} copy-done((bf16[1024,1664]{1,0:T(8,128)(2,1)S(1)}, bf16[1024,1664]{1,0:T(8,128)(2,1)}, u32[]{:S(2)}) %copy-start) | copy-done | bytes 3407896
  79.3 0.0 copy-start.1
  79.3 1.3 shard_map.87
  80.6 0.0 collective-permute-done.1.audio_ref
  80.6 0.6 copy-done.1
  81.3 1.3 %shard_map.88 = (f32[96,1024]{1,0:T(8,128)S(1)}, f32[32,1,1152]{2,1,0:T(1,128)S(1)}) custom-call(f32[1,1]{1,0:T(1,128)} %bitcast.2.scale_ref, bf16[192,1536]{1,0:T(8,128)(2,1)S(1)} %collective-permute-done.1.audio_ref, bf16[1024,1664]{1,0:T(8,128)(2,1)S(1)} %copy-done.1, f32[8,1024]{1,0:T(8,128)S(1)} %get-tuple-element.18.refs_0_), custom_call_target="tpu_custom_call" | custom-call | flops 603979776 | bytes 3407872 | tf_op jit(solution)/shard_map/pallas_call | solution.py:180
  82.6 17.7 %all_to_all.21.stats_ref = f32[32,1,1152]{2,1,0:T(1,128)S(1)} all-to-all(f32[32,1,1152]{2,1,0:T(1,128)S(1)} %get-tuple-element.19), channel_id=1, replica_groups=mesh['zl'=6,'y'=8,'c'=2,'zh'=2,'x'=4] {'y','x'}, dimensions={0} | all-to-all | bytes 294912 | tf_op jit(solution)/shard_map/all_to_all | solution.py:249
  100.3 0.0 copy-done.2
  100.3 1.4 %shard_map.89 = (f32[1,1024]{1,0:T(1,128)S(1)}, bf16[96,1536]{1,0:T(8,128)(2,1)S(1)}) custom-call(s32[96]{0:T(128)S(1)} %copy-done.2, f32[1,1]{1,0:T(1,128)} %bitcast.2.scale_ref, f32[32,1,1152]{2,1,0:T(1,128)S(1)} %all_to_all.21.stats_ref, f32[96,1024]{1,0:T(8,128)S(1)} %get-tuple-element.21.kept_ref, bf16[1024,1664]{1,0:T(8,128)(2,1)S(1)} %copy-done.1), custom_call_target="tpu_custom_call" | custom-call | flops 301989888 | bytes 3407872 | tf_op jit(solution)/shard_map/pallas_call | solution.py:180
  101.7 3.5 %collective-permute-start.2 = (bf16[96,1536]{1,0:T(8,128)(2,1)S(1)}, bf16[96,1536]{1,0:T(8,128)(2,1)S(1)}, u32[]{:S(2)}, u32[]{:S(2)}) collective-permute-start(bf16[96,1536]{1,0:T(8,128)(2,1)S(1)} %get-tuple-element.25), channel_id=1, source_target_pairs={{0,8},{8,0},{1,9},{9,1},{2,10},{10,2},{3,11},{11,3},{4,12},{12,4},... | collective-permute-start | bytes 884744 | tf_op jit(solution)/shard_map/ppermute | solution.py:27
  105.2 1.6 %shard_map.90 = (f32[1,16]{1,0:T(1,128)}, f32[96,1536]{1,0:T(8,128)S(1)}) custom-call(s32[96]{0:T(128)S(1)} %copy-done.2, f32[1,1]{1,0:T(1,128)} %bitcast.2.scale_ref, f32[32,1,1152]{2,1,0:T(1,128)S(1)} %all_to_all.21.stats_ref, f32[96,1024]{1,0:T(8,128)S(1)} %get-tuple-element.20.kept_ref, bf16[1024,1664]{1,0:T(8,128)(2,1)S(1)} %copy-done.1, ...), custom_call_target="tpu_custom_call" | custom-call | flops 301989888 | bytes 3407872 | tf_op jit(solution)/shard_map/pallas_call | solution.py:180
  106.8 0.0 collective-permute-done.2
  106.9 0.1 add_convert_fusion
  106.9 17.8 %all_to_all.22 = bf16[6,16,1536]{2,1,0:T(8,128)(2,1)S(1)} all-to-all(bf16[6,16,1536]{2,1,0:T(8,128)(2,1)S(1)} %bitcast.17), channel_id=1, replica_groups=mesh['zl'=6,'y'=8,'c'=2,'zh'=2,'x'=4] {'zl'}, dimensions={0} | all-to-all | bytes 589824 | tf_op jit(solution)/shard_map/all_to_all | solution.py:270
  124.7 0.7 convert_reduce_fusion.1
  (2 shorter events, 0.0 us)
Async XLA Ops:
  7.2 70.2 %all-gather.2.cloned.1.call-start = ((), (), s32[]{:S(2)}) async-start(), calls=%async_computation.4 | async-start | bytes 3833856 | tf_op jit(solution)/shard_map/all_gather | solution.py:221
  10.9 11.1 %all-to-all-start = ((bf16[4,2,16,1536]{3,2,1,0:T(8,128)(2,1)}), bf16[4,2,16,1536]{3,2,1,0:T(8,128)(2,1)S(1)}, u32[]{:S(2)}, u32[]{:S(2)}) async-start(bf16[4,2,16,1536]{3,2,1,0:T(8,128)(2,1)} %get-tuple-element.14), calls=%async_computation | async-start | bytes 786432 | tf_op jit(solution)/shard_map/all_to_all | solution.py:223
  22.1 17.0 %collective-permute-start = (bf16[16,1536]{1,0:T(8,128)(2,1)S(1)}, bf16[16,1536]{1,0:T(8,128)(2,1)S(1)}, u32[]{:S(2)}, u32[]{:S(2)}) collective-permute-start(bf16[16,1536]{1,0:T(8,128)(2,1)S(1)} %fusion), channel_id=1, source_target_pairs={{0,4},{4,0},{1,5},{5,1},{2,6},{6,2},{3,7},{7,3},{8,12},{12,8},{9,1... | collective-permute-start | bytes 147464 | tf_op jit(solution)/shard_map/ppermute | solution.py:27
  69.4 31.0 %copy-start.2 = (s32[96]{0:T(128)S(1)}, s32[96]{0:T(128)}, u32[]{:S(2)}) copy-start(s32[96]{0:T(128)} %count_ref.3) | copy-start | bytes 1156
  69.4 11.2 %collective-permute-start.1 = (bf16[192,1536]{1,0:T(8,128)(2,1)S(1)}, bf16[192,1536]{1,0:T(8,128)(2,1)S(1)}, u32[]{:S(2)}, u32[]{:S(2)}) collective-permute-start(bf16[192,1536]{1,0:T(8,128)(2,1)S(1)} %bitcast.14), channel_id=1, source_target_pairs={{0,8},{8,0},{1,9},{9,1},{2,10},{10,2},{3,11},{11,3},{4,12},{12,4},... | collective-permute-start | bytes 1769480 | tf_op jit(solution)/shard_map/ppermute | solution.py:27
  77.3 2.0 %copy-start = (bf16[1024,1664]{1,0:T(8,128)(2,1)S(1)}, bf16[1024,1664]{1,0:T(8,128)(2,1)}, u32[]{:S(2)}) copy-start(bf16[1024,1664]{1,0:T(8,128)(2,1)} %all-gather.2.cloned.1.call-done.text_ref) | copy-start | bytes 10223620
  79.3 2.0 %copy-start.1 = (bf16[1024,1664]{1,0:T(8,128)(2,1)S(1)}, bf16[1024,1664]{1,0:T(8,128)(2,1)}, u32[]{:S(2)}) copy-start(bf16[1024,1664]{1,0:T(8,128)(2,1)} %all-gather.2.cloned.1.call-done.text_ref) | copy-start | bytes 10223620
  101.7 5.1 %collective-permute-start.2 = (bf16[96,1536]{1,0:T(8,128)(2,1)S(1)}, bf16[96,1536]{1,0:T(8,128)(2,1)S(1)}, u32[]{:S(2)}, u32[]{:S(2)}) collective-permute-start(bf16[96,1536]{1,0:T(8,128)(2,1)S(1)} %get-tuple-element.25), channel_id=1, source_target_pairs={{0,8},{8,0},{1,9},{9,1},{2,10},{10,2},{3,11},{11,3},{4,12},{12,4},... | collective-permute-start | bytes 884744 | tf_op jit(solution)/shard_map/ppermute | solution.py:27
Sparse Core Ops, SparseCore 0:
  11.0 60.0 all-gather.1

commit v8 on v6

--- a/solution.py
+++ b/solution.py
@@ -46,7 +46,7 @@
     rows, width = text_ref.shape
     n_x, n_zh, share, _ = out_ref.shape
     depth = audio_ref.shape[1]
-    pieces = 4
+    pieces = 2
     spans = [pl.ds(i * depth // pieces, depth // pieces) for i in range(pieces)]
     pairs = [(text_hbm, text_ref), (pair_hbm, pair_ref)]
     for span in spans:
@@ -99,7 +99,6 @@
     rows = text_ref.shape[0] // n_y
     place = tuple(lax.axis_index(a) for a in BATCH + TENSOR)
     scale = scale_ref[...]
-    n_zl = audio_rows // (2 * share)
     step = 2 * rows
     zh = place[3]
     row_ids = lax.broadcasted_iota(I32, (audio_rows, step), 0)
@@ -108,16 +107,15 @@
         columns = []
         for i in range(2):
             held, column, near_c, pair_zh = pair_columns(text_ref, 2 * q + i, rows, width, place, sizes, share)
-            spot = lax.div(column, share) * 2 * share + lax.rem(column, share) + pair_zh * share
+            spot = column + pair_zh * kept_ref.shape[0]
             columns.append(jnp.where(held & (near_c == near), spot, -1))
         column = jnp.concatenate(columns, axis=1)
         part = scale * lax.dot_general(
             audio_ref[...], text_ref[span, :width], LAST, preferred_element_type=F32
         )
         picked = jnp.sum(jnp.where(row_ids == column, part, 0.0), axis=0, keepdims=True)
-        for zl in range(n_zl):
-            both = part[2 * zl * share : 2 * (zl + 1) * share]
-            kept_ref[zl * share : (zl + 1) * share, span] = jnp.where(zh == 0, both[:share], both[share:])
+        half = kept_ref.shape[0]
+        kept_ref[:, span] = jnp.where(zh == 0, part[:half], part[half:])
         top = jnp.max(part, axis=0, keepdims=True)
         if not before:
             stats_ref[0:1, span] = top
@@ -208,7 +206,7 @@
             pltpu.VMEM(audio_hidden.shape, BF16),
             pltpu.VMEM(head_in.shape[::-1], BF16),
             pltpu.VMEM(head_out.shape, BF16),
-            pltpu.SemaphoreType.DMA((11,)),
+            pltpu.SemaphoreType.DMA((7,)),
         ],
         flops=2 * rows * head_in.shape[1] * (head_in.shape[0] + width),
         moved=2 * (audio_hidden.size + head_in.size + head_out.size),
@@ -222,7 +220,7 @@
     raw = mine + swapped(other.astype(BF16), "zh").astype(F32)
     audio_unit = unit_rows(raw).astype(BF16)
 
-    own = spread(audio_unit, ("zl", "zh"), n_zl * n_zh).reshape(n_zl * n_zh * share, width)
+    own = spread(audio_unit, ("zh", "zl"), n_zl * n_zh).reshape(n_zl * n_zh * share, width)
     other = swapped(own, "c")
     half = n_zl * share
 

time: 133 us -> 133 us (level)
  no operation moved by 1% of the time
where the time goes in v8:
time: 133 us
  blocking collectives  64.9 us (49%)
  starting transfers between devices  32.6 us (25%)
  between operations  14.8 us (11%)
  Pallas kernels  8.29 us (6%)
  waiting for transfers between devices  8.26 us (6%)
  local copies, waits for them, and re-layouts  2.67 us (2%)
    all_to_all x1, blocking collectives, spread(): return lax.all_to_all(chunks, axis, 0, 0)  30.4 us
    ppermute x3, starting transfers between devices, swapped(): return lax.ppermute(value, axis, [(0, 1), (1, 0)])  27.7 us
    all_to_all x1, blocking collectives, on_device(): stats = lax.all_to_all(stats, ('y', 'x'), 0, 0)  17.7 us
    all_to_all x1, blocking collectives, on_device(): lax.all_to_all(near.astype(BF16).reshape(n_zl, share, width), 'zl', 0, 0)  16.8 us
    pallas_call x4, Pallas kernels, call(): pl.pallas_call(kernel, out_shape=outs, in_specs=specs, out_specs=jax.tree...  8.29 us
    all_to_all x1, waiting for transfers between devices, on_device(): lax.all_to_all(partial, 'x', 0, 0)  5.54 us
    all_to_all x1, starting transfers between devices, on_device(): lax.all_to_all(partial, 'x', 0, 0)  4.87 us
    ppermute x3, waiting for transfers between devices, swapped(): return lax.ppermute(value, axis, [(0, 1), (1, 0)])  2.69 us
  transfers between devices with their start and end apart: 5, of which 3 were waited for; matrix products, arithmetic and copies ran while one was open for 0% of the time, Pallas kernels for 1%

profile of v8, /device:TPU:1, one launch (start us, length us, event | category | flops | bytes accessed | tf_op | source)
XLA Modules:
  0.0 132.6 jit_solution(2947356857510321910)
XLA Ops:
  7.2 0.0 all-gather.2.cloned.1.call-start
  7.2 3.7 %shard_map.86 = (bf16[128,1664]{1,0:T(8,128)(2,1)}, bf16[4,2,16,1536]{3,2,1,0:T(8,128)(2,1)}) custom-call(bf16[128,1536]{1,0:T(8,128)(2,1)} %text_hbm.1, s32[1,128]{1,0:T(1,128)} %bitcast.18, bf16[128,4096]{1,0:T(8,128)(2,1)} %audio_hbm.1, bf16[192,4096]{1,0:T(8,128)(2,1)} %bitcast.16, bf16[192,1536]{1,0:T(8,128)(2,1)} %second_hbm.1), custom_call_target="tpu_custom_call" | custom-call | flops 276824064 | bytes 3211264 | tf_op jit(solution)/shard_map/pallas_call | solution.py:173
  10.9 0.0 all-gather.2.cloned.1.call-update
  11.0 4.9 %all-to-all-start = ((bf16[4,2,16,1536]{3,2,1,0:T(8,128)(2,1)}), bf16[4,2,16,1536]{3,2,1,0:T(8,128)(2,1)S(1)}, u32[]{:S(2)}, u32[]{:S(2)}) async-start(bf16[4,2,16,1536]{3,2,1,0:T(8,128)(2,1)} %get-tuple-element.13), calls=%async_computation | async-start | bytes 786432 | tf_op jit(solution)/shard_map/all_to_all | solution.py:216
  16.5 5.5 %all-to-all-done = bf16[4,2,16,1536]{3,2,1,0:T(8,128)(2,1)S(1)} async-done(((bf16[4,2,16,1536]{3,2,1,0:T(8,128)(2,1)}), bf16[4,2,16,1536]{3,2,1,0:T(8,128)(2,1)S(1)}, u32[]{:S(2)}, u32[]{:S(2)}) %all-to-all-start) | async-done | bytes 393248 | tf_op jit(solution)/shard_map/all_to_all | solution.py:216
  22.1 0.1 convert_reduce_fusion
  22.1 15.5 %collective-permute-start = (bf16[16,1536]{1,0:T(8,128)(2,1)S(1)}, bf16[16,1536]{1,0:T(8,128)(2,1)S(1)}, u32[]{:S(2)}, u32[]{:S(2)}) collective-permute-start(bf16[16,1536]{1,0:T(8,128)(2,1)S(1)} %fusion), channel_id=1, source_target_pairs={{0,4},{4,0},{1,5},{5,1},{2,6},{6,2},{3,7},{7,3},{8,12},{12,8},{9,1... | collective-permute-start | bytes 147464 | tf_op jit(solution)/shard_map/ppermute | solution.py:27
  37.6 1.5 %collective-permute-done = bf16[16,1536]{1,0:T(8,128)(2,1)S(1)} collective-permute-done((bf16[16,1536]{1,0:T(8,128)(2,1)S(1)}, bf16[16,1536]{1,0:T(8,128)(2,1)S(1)}, u32[]{:S(2)}, u32[]{:S(2)}) %collective-permute-start) | collective-permute-done | bytes 49184 | tf_op jit(solution)/shard_map/ppermute | solution.py:27
  39.1 0.1 multiply_reduce_fusion
  39.3 0.1 multiply_convert_fusion
  39.3 0.1 broadcast_in_dim.2
  39.4 30.4 %all_to_all.20 = bf16[12,16,1536]{2,1,0:T(8,128)(2,1)S(1)} all-to-all(bf16[12,16,1536]{2,1,0:T(8,128)(2,1)S(1)} %broadcast_in_dim.2), channel_id=1, replica_groups=mesh['zl'=6,'y'=8,'c'=2,'zh'=2,'x'=4] {'zh','zl'}, dimensions={0} | all-to-all | bytes 1179648 | tf_op jit(solution)/shard_map/all_to_all | solution.py:32
  69.8 0.0 copy-start.2
  69.8 8.7 %collective-permute-start.1 = (bf16[192,1536]{1,0:T(8,128)(2,1)S(1)}, bf16[192,1536]{1,0:T(8,128)(2,1)S(1)}, u32[]{:S(2)}, u32[]{:S(2)}) collective-permute-start(bf16[192,1536]{1,0:T(8,128)(2,1)S(1)} %bitcast.14), channel_id=1, source_target_pairs={{0,8},{8,0},{1,9},{9,1},{2,10},{10,2},{3,11},{11,3},{4,12},{12,4},... | collective-permute-start | bytes 1769480 | tf_op jit(solution)/shard_map/ppermute | solution.py:27
  78.6 0.0 all-gather.2.cloned.1.call-done.text_ref
  78.6 0.0 copy-start
  78.6 2.0 %copy-done = bf16[1024,1664]{1,0:T(8,128)(2,1)S(1)} copy-done((bf16[1024,1664]{1,0:T(8,128)(2,1)S(1)}, bf16[1024,1664]{1,0:T(8,128)(2,1)}, u32[]{:S(2)}) %copy-start) | copy-done | bytes 3407896
  80.6 0.0 copy-start.1
  80.6 1.3 shard_map.87
  81.9 0.0 collective-permute-done.1.audio_ref
  81.9 0.7 copy-done.1
  82.5 1.3 shard_map.88
  83.9 17.7 %all_to_all.21.stats_ref = f32[32,1,1152]{2,1,0:T(1,128)S(1)} all-to-all(f32[32,1,1152]{2,1,0:T(1,128)S(1)} %get-tuple-element.18), channel_id=1, replica_groups=mesh['zl'=6,'y'=8,'c'=2,'zh'=2,'x'=4] {'y','x'}, dimensions={0} | all-to-all | bytes 294912 | tf_op jit(solution)/shard_map/all_to_all | solution.py:242
  101.6 0.0 copy-done.2
  101.6 2.0 %shard_map.89 = (f32[1,16]{1,0:T(1,128)}, f32[96,1536]{1,0:T(8,128)S(1)}, bf16[96,1536]{1,0:T(8,128)(2,1)S(1)}) custom-call(s32[96]{0:T(128)S(1)} %copy-done.2, f32[1,1]{1,0:T(1,128)} %bitcast.2.scale_ref, f32[32,1,1152]{2,1,0:T(1,128)S(1)} %all_to_all.21.stats_ref, f32[96,1024]{1,0:T(8,128)S(1)} %get-tuple-element.19.own_ref, ...), custom_call_target="tpu_custom_call" | custom-call | flops 603979776 | bytes 3407872 | tf_op jit(solution)/shard_map/pallas_call | solution.py:173
  103.5 3.5 %collective-permute-start.2 = (bf16[96,1536]{1,0:T(8,128)(2,1)S(1)}, bf16[96,1536]{1,0:T(8,128)(2,1)S(1)}, u32[]{:S(2)}, u32[]{:S(2)}) collective-permute-start(bf16[96,1536]{1,0:T(8,128)(2,1)S(1)} %get-tuple-element.23), channel_id=1, source_target_pairs={{0,8},{8,0},{1,9},{9,1},{2,10},{10,2},{3,11},{11,3},{4,12},{12,4},... | collective-permute-start | bytes 884744 | tf_op jit(solution)/shard_map/ppermute | solution.py:27
  107.0 1.2 collective-permute-done.2
  108.2 0.1 add_convert_fusion
  108.3 16.8 %all_to_all.22 = bf16[6,16,1536]{2,1,0:T(8,128)(2,1)S(1)} all-to-all(bf16[6,16,1536]{2,1,0:T(8,128)(2,1)S(1)} %bitcast.17), channel_id=1, replica_groups=mesh['zl'=6,'y'=8,'c'=2,'zh'=2,'x'=4] {'zl'}, dimensions={0} | all-to-all | bytes 589824 | tf_op jit(solution)/shard_map/all_to_all | solution.py:258
  125.1 0.7 convert_reduce_fusion.1
  (2 shorter events, 0.0 us)
Async XLA Ops:
  7.2 71.4 %all-gather.2.cloned.1.call-start = ((), (), s32[]{:S(2)}) async-start(), calls=%async_computation.4 | async-start | bytes 3833856 | tf_op jit(solution)/shard_map/all_gather | solution.py:214
  11.0 11.1 %all-to-all-start = ((bf16[4,2,16,1536]{3,2,1,0:T(8,128)(2,1)}), bf16[4,2,16,1536]{3,2,1,0:T(8,128)(2,1)S(1)}, u32[]{:S(2)}, u32[]{:S(2)}) async-start(bf16[4,2,16,1536]{3,2,1,0:T(8,128)(2,1)} %get-tuple-element.13), calls=%async_computation | async-start | bytes 786432 | tf_op jit(solution)/shard_map/all_to_all | solution.py:216
  22.1 17.0 %collective-permute-start = (bf16[16,1536]{1,0:T(8,128)(2,1)S(1)}, bf16[16,1536]{1,0:T(8,128)(2,1)S(1)}, u32[]{:S(2)}, u32[]{:S(2)}) collective-permute-start(bf16[16,1536]{1,0:T(8,128)(2,1)S(1)} %fusion), channel_id=1, source_target_pairs={{0,4},{4,0},{1,5},{5,1},{2,6},{6,2},{3,7},{7,3},{8,12},{12,8},{9,1... | collective-permute-start | bytes 147464 | tf_op jit(solution)/shard_map/ppermute | solution.py:27
  69.8 31.7 %copy-start.2 = (s32[96]{0:T(128)S(1)}, s32[96]{0:T(128)}, u32[]{:S(2)}) copy-start(s32[96]{0:T(128)} %count_ref.1) | copy-start | bytes 1156
  69.8 12.0 %collective-permute-start.1 = (bf16[192,1536]{1,0:T(8,128)(2,1)S(1)}, bf16[192,1536]{1,0:T(8,128)(2,1)S(1)}, u32[]{:S(2)}, u32[]{:S(2)}) collective-permute-start(bf16[192,1536]{1,0:T(8,128)(2,1)S(1)} %bitcast.14), channel_id=1, source_target_pairs={{0,8},{8,0},{1,9},{9,1},{2,10},{10,2},{3,11},{11,3},{4,12},{12,4},... | collective-permute-start | bytes 1769480 | tf_op jit(solution)/shard_map/ppermute | solution.py:27
  78.6 2.0 %copy-start = (bf16[1024,1664]{1,0:T(8,128)(2,1)S(1)}, bf16[1024,1664]{1,0:T(8,128)(2,1)}, u32[]{:S(2)}) copy-start(bf16[1024,1664]{1,0:T(8,128)(2,1)} %all-gather.2.cloned.1.call-done.text_ref) | copy-start | bytes 10223620
  80.6 2.0 %copy-start.1 = (bf16[1024,1664]{1,0:T(8,128)(2,1)S(1)}, bf16[1024,1664]{1,0:T(8,128)(2,1)}, u32[]{:S(2)}) copy-start(bf16[1024,1664]{1,0:T(8,128)(2,1)} %all-gather.2.cloned.1.call-done.text_ref) | copy-start | bytes 10223620
  103.5 4.7 %collective-permute-start.2 = (bf16[96,1536]{1,0:T(8,128)(2,1)S(1)}, bf16[96,1536]{1,0:T(8,128)(2,1)S(1)}, u32[]{:S(2)}, u32[]{:S(2)}) collective-permute-start(bf16[96,1536]{1,0:T(8,128)(2,1)S(1)} %get-tuple-element.23), channel_id=1, source_target_pairs={{0,8},{8,0},{1,9},{9,1},{2,10},{10,2},{3,11},{11,3},{4,12},{12,4},... | collective-permute-start | bytes 884744 | tf_op jit(solution)/shard_map/ppermute | solution.py:27
Sparse Core Ops, SparseCore 0:
  11.1 60.0 all-gather.1
